TPU v7x, 512 devices: a whole 4x8x8 slice. The times are simulated.
512 devices in a mesh: dp: 64 (over x, z, core), tensor: 8 (over y).
Axes of the slice: x: 4, y: 8, z: 8, core: 2. Of those that a mesh axis runs over, the one named last changes fastest.
Arguments:
- queries: bfloat16 [32768, 4096], P('dp', 'tensor'), may hold values from -6 to 6
- keys: bfloat16 [32768, 1024], P('dp', 'tensor'), may hold values from -6 to 6
- values: bfloat16 [32768, 1024], P('dp', 'tensor'), may hold values from -6 to 6
- attn_out: bfloat16 [32768, 4096], P('dp', 'tensor'), may hold values from -6 to 6
- grad_out: bfloat16 [32768, 4096], P('dp', 'tensor'), may hold values from -24 to 24
- out_weight: bfloat16 [4096, 4096], P('dp', 'tensor'), may hold values from -0.09375 to 0.09375
- log_norm: float32 [32, 32768], P('tensor', 'dp')
- source_row: int32 [32768], P('dp'), may hold values from 0 to 32767, as said below
- dest_row: int32 [32768], P('dp'), may hold values from 0 to 32767, as said below
- slot_start: int32 [32768], P('dp'), may hold values from 0 to 32767, as said below
Outputs:
- grad_queries: bfloat16 [32768, 4096], P('dp', 'tensor')
- grad_keys: bfloat16 [32768, 1024], P('dp', 'tensor')
- grad_values: bfloat16 [32768, 1024], P('dp', 'tensor')
Inputs may be any that keep to these rules, and one draw needn't show every extreme that they name: `source_row`: a permutation of the packed positions; every document lies whole and in order within one device's block of 512 tokens in both orders; a balanced slot of device i of dp holds a token of device i - 1, i or i + 1 in packed order; across every boundary between neighbouring devices the same number of tokens moves each way, at least one and at most 72, exactly 72 at some boundary in every draw. `dest_row`: the inverse of source_row. `slot_start`: equal for all slots of one document; every document holds at most 400 tokens, and one holds exactly 400.
All inputs are finite; a program needn't handle non-finite values.
Results may differ from a plain program's by a relative error of at most 0.0063.
Values may be sent and summed in bfloat16 or wider, within the bound.
No kernel may reach another device: no remote copies, remote signals or barrier semaphores. Data moves between devices by JAX's collectives and lax.ppermute only.
A program may use at most 64 MiB of HBM per device.

v0:
```python
import jax
import jax.numpy as jnp
from jax import lax
from jax.sharding import PartitionSpec as P

HD = 128
GROUP = 4


def with_halo(block, sides, width):
    for axis, dim in sides:
        count = lax.axis_size(axis)
        forward = [(i, i + 1) for i in range(count - 1)]
        backward = [(target, source) for source, target in forward]
        low = lax.ppermute(
            lax.slice_in_dim(block, block.shape[dim] - width, None, axis=dim), axis, forward
        )
        high = lax.ppermute(lax.slice_in_dim(block, 0, width, axis=dim), axis, backward)
        block = jnp.concatenate([low, block, high], axis=dim)
    return block


def attend(queries, head_grads, window_keys, window_values, log_norm, row_delta, allowed, kv_count):
    row_count = queries.shape[0]
    key_count = window_keys.shape[0]
    query_heads = queries.reshape(row_count, kv_count, GROUP, HD)
    grad_heads = head_grads.reshape(row_count, kv_count, GROUP, HD)
    key_heads = window_keys.reshape(key_count, kv_count, HD)
    value_heads = window_values.reshape(key_count, kv_count, HD)
    norm_heads = log_norm.reshape(kv_count, GROUP, row_count)
    delta_heads = row_delta.reshape(kv_count, GROUP, row_count)
    scores = jnp.einsum(
        "pghe,jge->ghpj", query_heads, key_heads, preferred_element_type=jnp.float32
    ) * HD ** (-0.5)
    attn_prob = jnp.where(
        allowed[None, None], jnp.exp(scores - norm_heads[..., None]), jnp.float32(0.0)
    )
    grad_prob = jnp.einsum(
        "pghe,jge->ghpj", grad_heads, value_heads, preferred_element_type=jnp.float32
    )
    grad_score = attn_prob * (grad_prob - delta_heads[..., None])
    prob_half = attn_prob.astype(jnp.bfloat16)
    score_half = grad_score.astype(jnp.bfloat16)
    value_grad = jnp.einsum(
        "ghpj,pghe->jge", prob_half, grad_heads, preferred_element_type=jnp.float32
    )
    query_grad = jnp.einsum(
        "ghpj,jge->pghe", score_half, key_heads, preferred_element_type=jnp.float32
    )
    key_grad = jnp.einsum(
        "ghpj,pghe->jge", score_half, query_heads, preferred_element_type=jnp.float32
    )
    return (
        query_grad.reshape(row_count, -1),
        key_grad.reshape(key_count, -1),
        value_grad.reshape(key_count, -1),
    )


def on_device(
    queries,
    keys,
    values,
    attn_out,
    grad_out,
    out_weight,
    log_norm,
    source_row,
    dest_row,
    slot_start,
):
    row_count = queries.shape[0]
    query_width = queries.shape[1]
    key_width = keys.shape[1]
    kv_count = key_width // HD
    full_grad = lax.all_gather(grad_out, "tensor", axis=1, tiled=True)
    head_grads = jnp.dot(
        full_grad,
        lax.all_gather(out_weight, "dp", axis=0, tiled=True),
        preferred_element_type=jnp.float32,
    ).astype(jnp.bfloat16)
    packed = jnp.concatenate([queries, keys, values, head_grads], axis=1)
    first_row = lax.axis_index("dp") * row_count
    near_rows = with_halo(packed, (("dp", 0),), row_count)
    gathered = jnp.take(near_rows, source_row - first_row + row_count, axis=0)
    moved_queries = gathered[:, :query_width]
    moved_keys = gathered[:, query_width : query_width + key_width]
    moved_values = gathered[:, query_width + key_width : query_width + 2 * key_width]
    moved_grads = gathered[:, query_width + 2 * key_width :]
    product = moved_grads.astype(jnp.float32) * attn_out.astype(jnp.float32)
    row_delta = jnp.sum(product.reshape(row_count, -1, HD), axis=2).T
    allowed = (source_row[None, :] >= slot_start[:, None]) & (
        source_row[None, :] <= source_row[:, None]
    )
    query_grad, key_grad, value_grad = attend(
        moved_queries, moved_grads, moved_keys, moved_values, log_norm, row_delta, allowed, kv_count
    )
    attn_scale = HD ** (-0.5)
    back_rows = jnp.concatenate(
        [
            (query_grad * attn_scale).astype(jnp.bfloat16),
            (key_grad * attn_scale).astype(jnp.bfloat16),
            value_grad.astype(jnp.bfloat16),
        ],
        axis=1,
    )
    near_back = with_halo(back_rows, (("dp", 0),), row_count)
    result = jnp.take(near_back, dest_row - first_row + row_count, axis=0)
    grad_queries = result[:, :query_width]
    grad_keys = result[:, query_width : query_width + key_width]
    grad_values = result[:, query_width + key_width :]
    return (grad_queries, grad_keys, grad_values)


def solution(mesh):
    in_specs = (
        P("dp", "tensor"),
        P("dp", "tensor"),
        P("dp", "tensor"),
        P("dp", "tensor"),
        P("dp", "tensor"),
        P("dp", "tensor"),
        P("tensor", "dp"),
        P("dp"),
        P("dp"),
        P("dp"),
    )
    out_specs = (P("dp", "tensor"), P("dp", "tensor"), P("dp", "tensor"))
    return jax.shard_map(
        on_device, mesh=mesh, in_specs=in_specs, out_specs=out_specs, check_vma=False
    )
```

profile of v0, /device:TPU:2, one launch (start us, length us, event | category | flops | bytes accessed | tf_op | source)
XLA Modules:
  0.0 263.3 jit_solution(13445914736178598778)
XLA Ops:
  7.2 0.0 all-gather.3.cloned.1.call-start
  7.2 0.7 all-gather.3.cloned.1.call-update
  7.9 0.0 all-gather.5.cloned.1.call-start
  7.9 0.7 all-gather.5.cloned.1.call-update
  8.6 1.0 copy.44
  9.7 1.0 copy.43
  10.7 1.3 copy.42
  11.9 0.0 copy-start.4
  12.0 59.9 %all-gather.3.cloned.1.call-done = bf16[512,4096]{1,0:T(8,128)(2,1)} async-done(((bf16[512,512]{1,0:T(8,128)(2,1)}), bf16[512,4096]{1,0:T(8,128)(2,1)}) %all-gather.3.cloned.1.call-update) | async-done | bytes 4194320 | tf_op jit(solution)/shard_map/all_gather | solution.py:76
  71.9 86.5 %all-gather.5.cloned.1.call-done = bf16[4096,512]{1,0:T(8,128)(2,1)} async-done(((bf16[64,512]{1,0:T(8,128)(2,1)}), bf16[4096,512]{1,0:T(8,128)(2,1)}) %all-gather.5.cloned.1.call-update) | async-done | bytes 4194320 | tf_op jit(solution)/shard_map/all_gather | solution.py:79
  158.4 5.8 %convolution_convert_fusion = bf16[512,512]{0,1:T(8,128)(2,1)S(1)} fusion(bf16[512,4096]{1,0:T(8,128)(2,1)} %all-gather.3.cloned.1.call-done, bf16[4096,512]{1,0:T(8,128)(2,1)} %all-gather.5.cloned.1.call-done), kind=kOutput, calls=%fused_computation.22 | convolution fusion | flops 2147745792 | bytes 8912896 | tf_op jit(solution)/shard_map/dot_general | solution.py:77
  164.3 0.1 pad_maximum_fusion.2
  164.4 4.6 %collective-permute-start.1 = (bf16[512,1280]{0,1:T(8,128)(2,1)S(1)}, bf16[512,1280]{0,1:T(8,128)(2,1)}, u32[]{:S(2)}, u32[]{:S(2)}) collective-permute-start(bf16[512,1280]{0,1:T(8,128)(2,1)S(1)} %pad_maximum_fusion.2), channel_id=1, source_target_pairs={{8,0},{16,8},{24,16},{32,24},{40,32},{48,40},{56,48},{64,56},{72,6... | collective-permute-start | bytes 3932168 | tf_op jit(solution)/shard_map/ppermute | solution.py:18
  168.9 2.1 collective-permute-start
  171.1 0.3 compare_and_fusion
  171.4 12.7 %collective-permute-done.1 = bf16[512,1280]{0,1:T(8,128)(2,1)} collective-permute-done((bf16[512,1280]{0,1:T(8,128)(2,1)S(1)}, bf16[512,1280]{0,1:T(8,128)(2,1)}, u32[]{:S(2)}, u32[]{:S(2)}) %collective-permute-start.1) | collective-permute-done | bytes 1310752 | tf_op jit(solution)/shard_map/ppermute | solution.py:18
  184.0 6.0 %collective-permute-done = bf16[512,1280]{0,1:T(8,128)(2,1)} collective-permute-done((bf16[512,1280]{0,1:T(8,128)(2,1)S(1)}, bf16[512,1280]{0,1:T(8,128)(2,1)}, u32[]{:S(2)}, u32[]{:S(2)}) %collective-permute-start) | collective-permute-done | bytes 1310752 | tf_op jit(solution)/shard_map/ppermute | solution.py:15
  190.1 16.1 %pad_maximum_fusion = bf16[1536,1280]{0,1:T(8,128)(2,1)} fusion(bf16[512,1280]{0,1:T(8,128)(2,1)} %collective-permute-done.1, bf16[512,512]{0,1:T(8,128)(2,1)S(1)} %convolution_convert_fusion, bf16[512,128]{0,1:T(8,128)(2,1)S(1)} %copy.44, bf16[512,128]{0,1:T(8,128)(2,1)S(1)} %copy.43, bf16[512,512]{0,1:T(8,128)(2,1)S(1)} %copy.42, ...), kind=kLoop, calls=%fused_computation.8 | loop fusion | flops 23592960 | bytes 7864320 | tf_op jit(solution)/shard_map/concatenate | solution.py:19
  206.2 6.2 %copy.45 = bf16[1536,1280]{1,0:T(8,128)(2,1)} copy(bf16[1536,1280]{0,1:T(8,128)(2,1)} %pad_maximum_fusion) | data formatting | bytes 7864320 | tf_op jit(solution)/shard_map/concatenate | solution.py:19
  212.4 6.0 %gather_fusion = bf16[512,1280]{1,0:T(8,128)(2,1)S(1)} fusion(bf16[1536,1280]{1,0:T(8,128)(2,1)} %copy.45, s32[1024]{0:T(1024)S(1)} %pad_clamp_fusion.1), kind=kCustom, calls=%fused_computation | custom fusion | bytes 2623488 | tf_op jit(solution)/shard_map/jit(_take)/gather | solution.py:85
  218.3 0.2 broadcast_select_fusion
  218.5 0.1 fusion.43
  218.6 1.0 copy.64
  219.6 0.2 copy.46
  219.8 2.6 %fusion.40 = f32[512,512,4]{1,0,2:T(8,128)} fusion(bf16[512,4,128]{0,2,1:T(8,128)(2,1)S(1)} %bitcast.103, bf16[512,1280]{1,0:T(8,128)(2,1)S(1)} %broadcast_select_fusion), kind=kOutput, calls=%fused_computation.36 | convolution fusion | flops 268435456 | bytes 4849664 | tf_op jit(solution)/shard_map/pghe,jge->ghpj/dot_general | solution.py:32
  222.5 1.1 convert_multiply_fusion
  223.6 1.6 reshape.135
  225.2 0.6 reduce_sum.9
  225.8 0.0 copy-start.1
  225.8 0.1 copy.49
  225.9 3.6 %fusion.34 = bf16[512,128]{0,1:T(8,128)(2,1)S(1)} fusion(bf16[512,4,128]{0,2,1:T(8,128)(2,1)} %bitcast.107, f32[512,512,4]{1,0,2:T(8,128)} %fusion.40, f32[4,512]{1,0:T(4,128)S(1)} %copy-done.6, pred[512,512]{0,1:T(8,128)(4,1)S(1)} %compare_and_fusion), kind=kOutput, calls=%fused_computation.28 | convolution fusion | flops 272695296 | bytes 5120000 | tf_op jit(solution)/shard_map/ghpj,pghe->jge/dot_general | solution.py:44
  229.5 0.1 copy-done
  229.6 1.5 fusion.1
  231.1 0.8 fusion.37
  231.9 0.5 fusion.16
  232.4 0.1 copy.57
  232.5 0.1 copy.56
  232.7 0.2 copy.55
  232.9 0.1 pad_maximum_fusion.3
  233.0 1.9 collective-permute-start.3
  234.9 2.4 collective-permute-start.2
  237.3 7.0 %collective-permute-done.3 = bf16[512,768]{1,0:T(8,128)(2,1)S(1)} collective-permute-done((bf16[512,768]{1,0:T(8,128)(2,1)S(1)}, bf16[512,768]{1,0:T(8,128)(2,1)S(1)}, u32[]{:S(2)}, u32[]{:S(2)}) %collective-permute-start.3) | collective-permute-done | bytes 786464 | tf_op jit(solution)/shard_map/ppermute | solution.py:18
  244.4 5.9 %collective-permute-done.2 = bf16[512,768]{1,0:T(8,128)(2,1)S(1)} collective-permute-done((bf16[512,768]{1,0:T(8,128)(2,1)S(1)}, bf16[512,768]{1,0:T(8,128)(2,1)S(1)}, u32[]{:S(2)}, u32[]{:S(2)}) %collective-permute-start.2) | collective-permute-done | bytes 786464 | tf_op jit(solution)/shard_map/ppermute | solution.py:15
  250.3 0.6 pad_maximum_fusion.1
  250.9 2.7 %gather_fusion.1 = bf16[512,768]{1,0:T(8,128)(2,1)} fusion(bf16[1536,768]{1,0:T(8,128)(2,1)S(1)} %pad_maximum_fusion.1, s32[1024]{0:T(1024)S(1)} %pad_clamp_fusion), kind=kCustom, calls=%fused_computation.1 | custom fusion | bytes 1574912 | tf_op jit(solution)/shard_map/jit(_take)/gather | solution.py:108
  253.7 1.3 broadcast_select_fusion.1
  254.9 0.8 slice.36
  255.8 0.7 fusion.44
  (15 shorter events, 0.1 us)
Async XLA Ops:
  7.2 64.7 %all-gather.3.cloned.1.call-start = ((), (), s32[]{:S(2)}) async-start(), calls=%async_computation | async-start | bytes 4718592 | tf_op jit(solution)/shard_map/all_gather | solution.py:76
  7.9 150.5 %all-gather.5.cloned.1.call-start = ((), (), s32[]{:S(2)}) async-start(), calls=%async_computation.1 | async-start | bytes 4259840 | tf_op jit(solution)/shard_map/all_gather | solution.py:79
  11.9 159.1 %copy-start.3 = (s32[512]{0:T(512)S(1)}, s32[512]{0:T(512)}, u32[]{:S(2)}) copy-start(s32[512]{0:T(512)} %param.17) | copy-start | bytes 6148
  11.9 159.2 %copy-start.4 = (s32[512]{0:T(512)S(1)}, s32[512]{0:T(512)}, u32[]{:S(2)}) copy-start(s32[512]{0:T(512)} %param.19) | copy-start | bytes 6148
  164.4 19.7 %collective-permute-start.1 = (bf16[512,1280]{0,1:T(8,128)(2,1)S(1)}, bf16[512,1280]{0,1:T(8,128)(2,1)}, u32[]{:S(2)}, u32[]{:S(2)}) collective-permute-start(bf16[512,1280]{0,1:T(8,128)(2,1)S(1)} %pad_maximum_fusion.2), channel_id=1, source_target_pairs={{8,0},{16,8},{24,16},{32,24},{40,32},{48,40},{56,48},{64,56},{72,6... | collective-permute-start | bytes 3932168 | tf_op jit(solution)/shard_map/ppermute | solution.py:18
  168.9 21.1 %collective-permute-start = (bf16[512,1280]{0,1:T(8,128)(2,1)S(1)}, bf16[512,1280]{0,1:T(8,128)(2,1)}, u32[]{:S(2)}, u32[]{:S(2)}) collective-permute-start(bf16[512,1280]{0,1:T(8,128)(2,1)S(1)} %pad_maximum_fusion.2), channel_id=1, source_target_pairs={{0,8},{8,16},{16,24},{24,32},{32,40},{40,48},{48,56},{56,64},{64,7... | collective-permute-start | bytes 3932168 | tf_op jit(solution)/shard_map/ppermute | solution.py:15
  218.6 3.9 %copy-start.2 = (bf16[512,512]{1,0:T(8,128)(2,1)S(1)}, bf16[512,512]{1,0:T(8,128)(2,1)}, u32[]{:S(2)}) copy-start(bf16[512,512]{1,0:T(8,128)(2,1)} %param.13) | copy-start | bytes 1572868
  222.5 3.4 %copy-start.6 = (f32[4,512]{1,0:T(4,128)S(1)}, f32[4,512]{1,0:T(4,128)}, u32[]{:S(2)}) copy-start(f32[4,512]{1,0:T(4,128)} %param.16) | copy-start | bytes 24580
  225.8 3.7 %copy-start.1 = (bf16[512,512]{0,1:T(8,128)(2,1)S(1)}, bf16[512,512]{0,1:T(8,128)(2,1)}, u32[]{:S(2)}) copy-start(bf16[512,512]{0,1:T(8,128)(2,1)} %copy.64) | copy-start | bytes 1572868
  225.9 3.7 %copy-start = (f32[512,512,4]{1,0,2:T(8,128)S(1)}, f32[512,512,4]{1,0,2:T(8,128)}, u32[]{:S(2)}) copy-start(f32[512,512,4]{1,0,2:T(8,128)} %fusion.40) | copy-start | bytes 12582916
  231.1 6.2 %copy-start.5 = (s32[512]{0:T(512)S(1)}, s32[512]{0:T(512)}, u32[]{:S(2)}) copy-start(s32[512]{0:T(512)} %param.18) | copy-start | bytes 6148
  233.0 11.4 %collective-permute-start.3 = (bf16[512,768]{1,0:T(8,128)(2,1)S(1)}, bf16[512,768]{1,0:T(8,128)(2,1)S(1)}, u32[]{:S(2)}, u32[]{:S(2)}) collective-permute-start(bf16[512,768]{1,0:T(8,128)(2,1)S(1)} %pad_maximum_fusion.3), channel_id=1, source_target_pairs={{8,0},{16,8},{24,16},{32,24},{40,32},{48,40},{56,48},{64,56},{72,6... | collective-permute-start | bytes 2359304 | tf_op jit(solution)/shard_map/ppermute | solution.py:18
  234.9 15.4 %collective-permute-start.2 = (bf16[512,768]{1,0:T(8,128)(2,1)S(1)}, bf16[512,768]{1,0:T(8,128)(2,1)S(1)}, u32[]{:S(2)}, u32[]{:S(2)}) collective-permute-start(bf16[512,768]{1,0:T(8,128)(2,1)S(1)} %pad_maximum_fusion.3), channel_id=1, source_target_pairs={{0,8},{8,16},{16,24},{24,32},{32,40},{40,48},{48,56},{56,64},{64,7... | collective-permute-start | bytes 2359304 | tf_op jit(solution)/shard_map/ppermute | solution.py:15
Sparse Core Ops, SparseCore 0:
  10.1 61.7 all-gather.2
  75.2 83.1 all-gather.4
where the time goes:
time: 264 us; the launch traced here: 263 us
  waiting for transfers between devices  180 us (68%)
  local copies, waits for them, and re-layouts  23.2 us (9%)
  other arithmetic  20.4 us (8%)
  matrix products  14.8 us (6%)
  between operations  14.3 us (5%)
  starting transfers between devices  11.1 us (4%)
    all_gather x1, waiting for transfers between devices, on_device(): lax.all_gather(out_weight, 'dp', axis=0, tiled=True)  86.5 us
    all_gather x1, waiting for transfers between devices, on_device(): full_grad = lax.all_gather(grad_out, 'tensor', axis=1, tiled=True)  59.9 us
    ppermute x2, waiting for transfers between devices, with_halo(): lax.ppermute(lax.slice_in_dim(block, 0, width, axis=dim), axis, backward)  19.7 us
    concatenate x2, other arithmetic, with_halo(): block = jnp.concatenate([low, block, high], axis=dim)  16.7 us
    ppermute x2, waiting for transfers between devices, with_halo(): lax.ppermute(lax.slice_in_dim(block, block.shape[dim] - width, None, axis...  12 us
    ppermute x2, starting transfers between devices, with_halo(): lax.ppermute(lax.slice_in_dim(block, 0, width, axis=dim), axis, backward)  6.5 us
    concatenate x1, local copies, waits for them, and re-layouts, with_halo(): block = jnp.concatenate([low, block, high], axis=dim)  6.15 us
    gather x1, local copies, waits for them, and re-layouts, on_device(): gathered = jnp.take(near_rows, source_row - first_row + row_count, axis=0)  5.96 us
  transfers between devices with their start and end apart: 6, of which 6 were waited for; matrix products, arithmetic and copies ran while one was open for 1% of the time, Pallas kernels for 0%

commit v1 on v0

v1 whole, which is shorter than its diff:
```python
import jax
import jax.numpy as jnp
from jax import lax
from jax.experimental import pallas as pl
from jax.experimental.pallas import tpu as pltpu
from jax.sharding import PartitionSpec as P

HD = 128
GROUP = 4
HALO = 80
BLK = 256
X, Z = 4, 8

NT = (((1,), (1,)), ((), ()))
TN = (((0,), (0,)), ((), ()))


def dot(a, b, dims=(((1,), (0,)), ((), ()))):
    return lax.dot_general(a, b, dims, preferred_element_type=jnp.float32)


def iota(shape, dim):
    return lax.broadcasted_iota(jnp.int32, shape, dim)


def send_kernel(first_ref, source_ref, start_ref, norm_ref, attn_ref, left_ref, right_ref, stats_ref, parts):
    first = first_ref[0]
    rows, width = attn_ref.shape
    source = source_ref[...]
    is_left = source < first
    is_right = source >= first + rows
    parts[...] = jnp.zeros_like(parts)
    rest = norm_ref[...]
    for part in range(3):
        half = rest.astype(jnp.bfloat16).astype(jnp.float32)
        parts[8 * part : 8 * part + GROUP, :] = half
        rest = rest - half
    start = start_ref[...]
    parts[24:25, :] = (start // 128).astype(jnp.float32)
    parts[32:33, :] = (start % 128).astype(jnp.float32)
    stats_ref[...] = parts[...].astype(jnp.bfloat16)
    until = (iota((rows, rows), 0) <= iota((rows, rows), 1)).astype(jnp.bfloat16)
    for mask, out_ref in ((is_left, left_ref), (is_right, right_ref)):
        flags = jnp.broadcast_to(jnp.where(mask, 1.0, 0.0), (16, rows))
        count = dot(flags.astype(jnp.bfloat16), until)[:1].astype(jnp.int32)
        place = jnp.where(mask, count - 1, -1)
        pick = jnp.where(iota((HALO, rows), 0) == place, 1.0, 0.0).astype(jnp.bfloat16)
        out_ref[:, :width] = dot(pick, attn_ref[...]).astype(jnp.bfloat16)
        out_ref[:, width:] = dot(pick, stats_ref[...], NT).astype(jnp.bfloat16)


def receive_kernel(first_ref, dest_ref, attn_ref, stats_ref, low_ref, high_ref, attn_out_ref, stats_out_ref):
    first = first_ref[0].astype(jnp.float32)
    rows, width = attn_ref.shape
    dest_row = dest_ref[...].astype(jnp.float32)
    dest_col = jnp.broadcast_to(dest_row, (128, rows)).T[:, :1]
    smaller = jnp.sum(jnp.where(dest_row < dest_col, 1.0, 0.0), axis=1, keepdims=True)
    below_high = jnp.sum(jnp.where(dest_row < first + rows, 1.0, 0.0), axis=1, keepdims=True)
    place_low = jnp.where(dest_col < first, smaller, -1.0).astype(jnp.int32)
    place_high = jnp.where(dest_col >= first + rows, smaller - below_high, -1.0).astype(jnp.int32)
    place_here = (dest_col - first).astype(jnp.int32)
    here = jnp.where(iota((rows, rows), 1) == place_here, 1.0, 0.0).astype(jnp.bfloat16)
    low = jnp.where(iota((rows, HALO), 1) == place_low, 1.0, 0.0).astype(jnp.bfloat16)
    high = jnp.where(iota((rows, HALO), 1) == place_high, 1.0, 0.0).astype(jnp.bfloat16)
    moved = dot(here, attn_ref[...]) + dot(low, low_ref[:, :width]) + dot(high, high_ref[:, :width])
    attn_out_ref[...] = moved.astype(jnp.bfloat16)
    stats_t = (
        dot(stats_ref[...], here, NT)
        + dot(low_ref[:, width:].T, low, NT)
        + dot(high_ref[:, width:].T, high, NT)
    )
    stats_out_ref[0:8, :] = stats_t[0:8] + stats_t[8:16] + stats_t[16:24]
    stats_out_ref[8:16, :] = stats_t[24:32] * 128.0 + stats_t[32:40] - first


def tiles_of(rows):
    return [(i, j) for i in range(rows // BLK) for j in range(i + 1)]


def attend_kernel(
    me_ref, grad_ref, near_ref, far_ref, near_other_ref, far_other_ref,
    query_in, key_in, value_in, attn_in, stats_in,
    dq_ref, dk_ref, dv_ref,
    grad_buf, weight_buf, query_ref, key_ref, value_ref, attn_ref, stats_ref,
    total, prob, heads, grad_sems, weight_sems, sems,
):
    parts, rows, depth = grad_ref.shape
    scale = HD**-0.5
    my_x, my_z, my_core = me_ref[0], me_ref[1], me_ref[2]
    ins = [
        pltpu.make_async_copy(source, target, sems.at[index])
        for index, (source, target) in enumerate(
            ((query_in, query_ref), (key_in, key_ref), (stats_in, stats_ref), (value_in, value_ref), (attn_in, attn_ref))
        )
    ]
    for copy in ins:
        copy.start()
    for refs, core in (((near_ref, far_ref), my_core), ((near_other_ref, far_other_ref), 1 - my_core)):
        for piece_ref, z_steps in zip(refs, (NEAR, FAR)):
            for index, step in enumerate(z_steps):
                z = lax.rem(my_z + step + Z, Z)
                pltpu.make_async_copy(
                    piece_ref.at[index], weight_buf.at[z, :, core], weight_sems.at[2 * z + core]
                ).start()
    grads = []
    for half in range(2):
        for index, step in enumerate(COLUMN):
            part = 2 * (my_x ^ step) + half
            copy = pltpu.make_async_copy(grad_ref.at[part], grad_buf.at[index, half], grad_sems.at[index, half])
            copy.start()
            grads.append(copy)
    for copy in ins[:3]:
        copy.wait()
    for i, j in tiles_of(rows):
        tokens, others = pl.ds(i * BLK, BLK), pl.ds(j * BLK, BLK)
        begin = stats_ref[8:9, tokens].astype(jnp.int32)
        other = iota((BLK, BLK), 0) + j * BLK
        token = iota((BLK, BLK), 1) + i * BLK
        allowed = (begin <= other) & (other <= token)
        for h in range(GROUP):
            score = dot(key_ref[others, :], query_ref[tokens, h * HD : (h + 1) * HD], NT) * scale
            prob[h, others, tokens] = jnp.where(allowed, jnp.exp(score - stats_ref[h : h + 1, tokens]), 0.0)
    for z in range(Z):
        half, place = z // (Z // 2), z % (Z // 2)
        for core in range(2):
            pltpu.make_async_copy(near_ref.at[0], weight_buf.at[z, :, core], weight_sems.at[2 * z + core]).wait()
        if place == 0:
            for copy in grads[half * X : (half + 1) * X]:
                copy.wait()
        left = jnp.concatenate([grad_buf[x, half, :, place * 128 : (place + 1) * 128] for x in range(X)], axis=1)
        product = dot(left, weight_buf[z].reshape(depth, -1))
        if z == 0:
            total[...] = product
        else:
            total[...] += product
    for copy in ins[3:]:
        copy.wait()
    heads[...] = total[...].astype(jnp.bfloat16)
    delta = jnp.zeros((rows, HD), jnp.float32)
    for h in range(GROUP):
        cols = slice(h * HD, (h + 1) * HD)
        product = heads[:, cols].astype(jnp.float32) * attn_ref[:, cols].astype(jnp.float32)
        delta = jnp.where(iota((rows, HD), 1) == h, jnp.sum(product, axis=1, keepdims=True), delta)
    delta = delta.T
    key_total = [0.0] * (rows // BLK)
    value_total = [0.0] * (rows // BLK)
    query_total = {}
    for i, j in tiles_of(rows):
        tokens, others = pl.ds(i * BLK, BLK), pl.ds(j * BLK, BLK)
        for h in range(GROUP):
            cols = slice(h * HD, (h + 1) * HD)
            grads = heads[tokens, cols]
            p = prob[h, others, tokens]
            grad_prob = dot(value_ref[others, :], grads, NT)
            grad_score = p * (grad_prob - delta[h : h + 1, i * BLK : (i + 1) * BLK])
            score_half = grad_score.astype(jnp.bfloat16)
            value_total[j] += dot(p.astype(jnp.bfloat16), grads)
            key_total[j] += dot(score_half, query_ref[tokens, cols])
            update = dot(score_half, key_ref[others, :], TN)
            query_total[i, h] = query_total[i, h] + update if (i, h) in query_total else update
    for (i, h), value in query_total.items():
        dq_ref[pl.ds(i * BLK, BLK), h * HD : (h + 1) * HD] = (value * scale).astype(jnp.bfloat16)
    for j in range(rows // BLK):
        dk_ref[pl.ds(j * BLK, BLK), :] = (key_total[j] * scale).astype(jnp.bfloat16)
        dv_ref[pl.ds(j * BLK, BLK), :] = value_total[j].astype(jnp.bfloat16)


def move(block, target):
    pairs = []
    for x in range(X):
        for z in range(Z):
            for core in range(2):
                tx, tz, tc = target(x, z, core)
                pairs.append(((x * Z + z) * 2 + core, ((tx % X) * Z + tz % Z) * 2 + tc))
    return lax.ppermute(block, "dp", pairs)


SMEM = pl.BlockSpec(memory_space=pltpu.SMEM)
VMEM = pl.BlockSpec(memory_space=pltpu.VMEM)
HBM = pl.BlockSpec(memory_space=pltpu.HBM)


def after(value, *others):
    return lax.optimization_barrier((value, *others))[0]


COLUMN = (0, 1, 3, 2)
NEAR, FAR = (0, -1, 1, -2, 2), (-3, 3, 4)


def on_device(
    queries, keys, values, attn_out, grad_out, out_weight, log_norm, source_row, dest_row, slot_start
):
    rows, width = queries.shape
    key_width = keys.shape[1]
    all_grad = lax.all_gather(grad_out, "tensor", axis=0, tiled=False)

    me = lax.axis_index("dp").astype(jnp.int32)
    first = (me * rows).reshape(1)
    place = jnp.stack([me // (2 * Z), (me // 2) % Z, me % 2])
    message = jax.ShapeDtypeStruct((HALO, width + 128), jnp.bfloat16)
    to_low, to_high, stats = pl.pallas_call(
        send_kernel,
        out_shape=(message, message, jax.ShapeDtypeStruct((128, rows), jnp.bfloat16)),
        in_specs=[SMEM] + [VMEM] * 4,
        out_specs=(VMEM,) * 3,
        scratch_shapes=[pltpu.VMEM((128, rows), jnp.float32)],
        cost_estimate=pl.CostEstimate(flops=2 * 2 * HALO * rows * 640, bytes_accessed=1 << 20, transcendentals=0),
        name="send_rows",
    )(first, source_row[None], slot_start[None], log_norm, attn_out)

    up = lambda x, z, c: (x, z + 1, c)
    down = lambda x, z, c: (x, z - 1, c)
    other = lambda x, z, c: (x, z, 1 - c)
    pair = jnp.concatenate([out_weight, move(out_weight, lambda x, z, c: (x ^ 1, z, c))], axis=0)
    pair = after(pair, to_low, to_high)
    forward = [(i, i + 1) for i in range(lax.axis_size("dp") - 1)]
    from_low = lax.ppermute(to_high, "dp", forward)
    from_high = lax.ppermute(to_low, "dp", [(b, a) for a, b in forward])
    column = jnp.concatenate([pair, move(pair, lambda x, z, c: (3 - x, z, c))], axis=0)
    up1 = move(column, up)
    attn_packed, stats_packed = pl.pallas_call(
        receive_kernel,
        out_shape=(
            jax.ShapeDtypeStruct((rows, width), jnp.bfloat16),
            jax.ShapeDtypeStruct((16, rows), jnp.float32),
        ),
        in_specs=[SMEM] + [VMEM] * 5,
        out_specs=(VMEM, VMEM),
        cost_estimate=pl.CostEstimate(flops=2 * rows * rows * 640, bytes_accessed=2 << 20, transcendentals=0),
        name="receive_rows",
    )(first, dest_row[None], attn_out, stats, from_low, from_high)
    down1 = move(column, down)
    up2, down2 = move(up1, up), move(after(down1, attn_packed, stats_packed), down)
    up3, down3 = move(up2, up), move(down2, down)
    up4 = move(up3, up)
    near = jnp.concatenate([column, up1, down1, up2, down2], axis=0)
    near_other = move(near, other)
    far = jnp.concatenate([up3, down3, up4], axis=0)
    far_other = move(far, other)
    pieces = [piece.reshape(-1, X, *out_weight.shape) for piece in (near, far, near_other, far_other)]

    parts, _, depth = all_grad.shape
    return pl.pallas_call(
        attend_kernel,
        out_shape=(
            jax.ShapeDtypeStruct((rows, width), jnp.bfloat16),
            jax.ShapeDtypeStruct((rows, key_width), jnp.bfloat16),
            jax.ShapeDtypeStruct((rows, key_width), jnp.bfloat16),
        ),
        in_specs=[SMEM] + [HBM] * 10,
        out_specs=(VMEM, VMEM, VMEM),
        scratch_shapes=[
            pltpu.VMEM((X, 2, rows, depth), jnp.bfloat16),
            pltpu.VMEM((Z, X, 2, *out_weight.shape), jnp.bfloat16),
            pltpu.VMEM(queries.shape, jnp.bfloat16),
            pltpu.VMEM(keys.shape, jnp.bfloat16),
            pltpu.VMEM(values.shape, jnp.bfloat16),
            pltpu.VMEM(attn_out.shape, jnp.bfloat16),
            pltpu.VMEM(stats_packed.shape, jnp.float32),
            pltpu.VMEM((rows, width), jnp.float32),
            pltpu.VMEM((GROUP, rows, rows), jnp.float32),
            pltpu.VMEM((rows, width), jnp.bfloat16),
            pltpu.SemaphoreType.DMA((X, 2)),
            pltpu.SemaphoreType.DMA((2 * Z,)),
            pltpu.SemaphoreType.DMA((5,)),
        ],
        compiler_params=pltpu.CompilerParams(vmem_limit_bytes=60 << 20),
        cost_estimate=pl.CostEstimate(flops=4 << 30, bytes_accessed=12 << 20, transcendentals=1 << 20),
        name="attend",
    )(place, all_grad, *pieces, queries, keys, values, attn_packed, stats_packed)


def solution(mesh):
    in_specs = (P("dp", "tensor"),) * 6 + (P("tensor", "dp"), P("dp"), P("dp"), P("dp"))
    out_specs = (P("dp", "tensor"),) * 3
    return jax.shard_map(
        on_device, mesh=mesh, in_specs=in_specs, out_specs=out_specs, check_vma=False
    )
```

time: 264 us -> 101 us (0.38)
  the two profiles are of different devices: /device:TPU:2 before, /device:TPU:1 now
where the time goes in v1:
time: 101 us; the launch traced here: 100 us
  starting transfers between devices  49.6 us (49%)
  Pallas kernels  16.6 us (16%)
  waiting for transfers between devices  16.2 us (16%)
  between operations  14.3 us (14%)
  local copies, waits for them, and re-layouts  1.77 us (2%)
  other arithmetic  1.52 us (2%)
    ppermute x11, starting transfers between devices, move(): return lax.ppermute(block, 'dp', pairs)  43 us
    ppermute x11, waiting for transfers between devices, move(): return lax.ppermute(block, 'dp', pairs)  15.5 us
    pallas_call x1, Pallas kernels, on_device(): pl.pallas_call(attend_kernel, out_shape=(jax.ShapeDtypeStruct((rows, widt...  10.5 us
    ppermute x1, starting transfers between devices, on_device(): from_high = lax.ppermute(to_low, 'dp', [(b, a) for a, b in forward])  4.69 us
    pallas_call x1, Pallas kernels, on_device(): pl.pallas_call(receive_kernel, out_shape=(jax.ShapeDtypeStruct((rows, wid...  3.47 us
    pallas_call x1, Pallas kernels, on_device(): pl.pallas_call(send_kernel, out_shape=(message, message, jax.ShapeDtypeSt...  2.55 us
  transfers between devices with their start and end apart: 14, of which 5 were waited for; matrix products, arithmetic and copies ran while one was open for 2% of the time, Pallas kernels for 6%

profile of v1, /device:TPU:1, one launch (start us, length us, event | category | flops | bytes accessed | tf_op | source)
XLA Modules:
  0.0 100.0 jit_solution(5013049616498593266)
XLA Ops:
  7.2 0.0 all-gather.3.cloned.1.call-start
  7.2 0.7 all-gather.3.cloned.1.call-update
  7.9 4.0 %collective-permute-start = (bf16[64,512]{1,0:T(8,128)(2,1)}, bf16[64,512]{1,0:T(8,128)(2,1)S(1)}, u32[]{:S(2)}, u32[]{:S(2)}) collective-permute-start(bf16[64,512]{1,0:T(8,128)(2,1)} %param.15), channel_id=1, source_target_pairs={{0,128},{8,136},{16,144},{24,152},{32,160},{40,168},{48,176},{56,1... | collective-permute-start | bytes 196616 | tf_op jit(solution)/shard_map/ppermute | solution.py:175
  11.9 2.6 %send_rows.1 = (bf16[80,640]{1,0:T(8,128)(2,1)}, bf16[80,640]{1,0:T(8,128)(2,1)}, bf16[128,512]{1,0:T(8,128)(2,1)}) custom-call(s32[1]{0:T(128)} %bitcast.4.first_ref, s32[1,512]{1,0:T(1,128)} %bitcast.14, s32[1,512]{1,0:T(1,128)} %bitcast.15, f32[4,512]{1,0:T(4,128)} %norm_ref.1, bf16[512,512]{1,0:T(8,128)(2,1)} %attn_ref.3), custom_call_target="tpu_custom_call" | custom-call | flops 104857600 | bytes 1048576 | tf_op jit(solution)/shard_map/send_rows/pallas_call | solution.py:202
  14.4 0.0 collective-permute-done
  14.4 0.8 pad_maximum_fusion
  15.3 3.9 %collective-permute-start.1 = (bf16[128,512]{1,0:T(8,128)(2,1)S(1)}, bf16[128,512]{1,0:T(8,128)(2,1)S(1)}, u32[]{:S(2)}, u32[]{:S(2)}) collective-permute-start(bf16[128,512]{1,0:T(8,128)(2,1)S(1)} %pad_maximum_fusion), channel_id=1, source_target_pairs={{0,384},{8,392},{16,400},{24,408},{32,416},{40,424},{48,432},{56,4... | collective-permute-start | bytes 393224 | tf_op jit(solution)/shard_map/ppermute | solution.py:175
  19.2 3.0 %collective-permute-done.1 = bf16[128,512]{1,0:T(8,128)(2,1)S(1)} collective-permute-done((bf16[128,512]{1,0:T(8,128)(2,1)S(1)}, bf16[128,512]{1,0:T(8,128)(2,1)S(1)}, u32[]{:S(2)}, u32[]{:S(2)}) %collective-permute-start.1) | collective-permute-done | bytes 131104 | tf_op jit(solution)/shard_map/ppermute | solution.py:175
  22.2 4.0 %collective-permute-start.2 = (bf16[256,512]{1,0:T(8,128)(2,1)S(1)}, bf16[256,512]{1,0:T(8,128)(2,1)S(1)}, u32[]{:S(2)}, u32[]{:S(2)}) collective-permute-start(bf16[256,512]{1,0:T(8,128)(2,1)S(1)} %get-tuple-element.17), channel_id=1, source_target_pairs={{0,16},{8,24},{16,32},{24,40},{32,48},{40,56},{48,64},{56,72},{64,... | collective-permute-start | bytes 786440 | tf_op jit(solution)/shard_map/ppermute | solution.py:175
  26.2 8.6 %collective-permute-start.3 = (bf16[256,512]{1,0:T(8,128)(2,1)S(1)}, bf16[256,512]{1,0:T(8,128)(2,1)S(1)}, u32[]{:S(2)}, u32[]{:S(2)}) collective-permute-start(bf16[256,512]{1,0:T(8,128)(2,1)S(1)} %get-tuple-element.17), channel_id=1, source_target_pairs={{0,112},{8,120},{16,0},{24,8},{32,16},{40,24},{48,32},{56,40},{64,... | collective-permute-start | bytes 786440 | tf_op jit(solution)/shard_map/ppermute | solution.py:175
  34.8 4.7 %collective-permute-start.6 = (bf16[80,640]{1,0:T(8,128)(2,1)}, bf16[80,640]{1,0:T(8,128)(2,1)S(1)}, u32[]{:S(2)}, u32[]{:S(2)}) collective-permute-start(bf16[80,640]{1,0:T(8,128)(2,1)} %get-tuple-element.10), channel_id=1, source_target_pairs={{8,0},{16,8},{24,16},{32,24},{40,32},{48,40},{56,48},{64,56},{72,6... | collective-permute-start | bytes 307208 | tf_op jit(solution)/shard_map/ppermute | solution.py:219
  39.5 1.9 %collective-permute-start.5 = (bf16[80,640]{1,0:T(8,128)(2,1)}, bf16[80,640]{1,0:T(8,128)(2,1)S(1)}, u32[]{:S(2)}, u32[]{:S(2)}) collective-permute-start(bf16[80,640]{1,0:T(8,128)(2,1)} %get-tuple-element.11), channel_id=1, source_target_pairs={{0,8},{8,16},{16,24},{24,32},{32,40},{40,48},{48,56},{56,64},{64,7... | collective-permute-start | bytes 307208 | tf_op jit(solution)/shard_map/ppermute | solution.py:218
  41.5 0.0 collective-permute-done.2
  41.5 1.9 %collective-permute-start.4 = (bf16[256,512]{1,0:T(8,128)(2,1)S(1)}, bf16[256,512]{1,0:T(8,128)(2,1)S(1)}, u32[]{:S(2)}, u32[]{:S(2)}) collective-permute-start(bf16[256,512]{1,0:T(8,128)(2,1)S(1)} %collective-permute-done.2), channel_id=1, source_target_pairs={{0,16},{8,24},{16,32},{24,40},{32,48},{40,56},{48,64},{56,72},{64,... | collective-permute-start | bytes 786440 | tf_op jit(solution)/shard_map/ppermute | solution.py:175
  43.4 0.0 collective-permute-done.6.high_ref
  43.4 0.0 copy-start.3
  43.4 0.0 collective-permute-done.5.low_ref
  43.4 0.0 copy-start.4
  43.4 0.6 copy-done.3
  44.0 0.0 copy-done.4
  44.1 3.5 %receive_rows.1 = (bf16[512,512]{1,0:T(8,128)(2,1)}, f32[16,512]{1,0:T(8,128)}) custom-call(s32[1]{0:T(128)} %bitcast.4.first_ref, s32[1,512]{1,0:T(1,128)} %bitcast.18, bf16[512,512]{1,0:T(8,128)(2,1)} %attn_ref.3, bf16[128,512]{1,0:T(8,128)(2,1)} %get-tuple-element.13.stats_ref, bf16[80,640]{1,0:T(8,128)(2,1)} %copy-done.4, bf16[80,640]{1,0:T(8,128)(2,1)} %copy-done.3), custom_call_target="tpu_custom_call" | custom-call | flops 335544320 | bytes 2097152 | tf_op jit(solution)/shard_map/receive_rows/pallas_call | solution.py:222
  47.6 0.0 collective-permute-done.3
  47.6 4.6 %collective-permute-start.7 = (bf16[256,512]{1,0:T(8,128)(2,1)S(1)}, bf16[256,512]{1,0:T(8,128)(2,1)S(1)}, u32[]{:S(2)}, u32[]{:S(2)}) collective-permute-start(bf16[256,512]{1,0:T(8,128)(2,1)S(1)} %collective-permute-done.3), channel_id=1, source_target_pairs={{0,112},{8,120},{16,0},{24,8},{32,16},{40,24},{48,32},{56,40},{64,... | collective-permute-start | bytes 786440 | tf_op jit(solution)/shard_map/ppermute | solution.py:175
  52.2 0.0 collective-permute-done.4
  52.2 1.9 %collective-permute-start.8 = (bf16[256,512]{1,0:T(8,128)(2,1)S(1)}, bf16[256,512]{1,0:T(8,128)(2,1)S(1)}, u32[]{:S(2)}, u32[]{:S(2)}) collective-permute-start(bf16[256,512]{1,0:T(8,128)(2,1)S(1)} %collective-permute-done.4), channel_id=1, source_target_pairs={{0,16},{8,24},{16,32},{24,40},{32,48},{40,56},{48,64},{56,72},{64,... | collective-permute-start | bytes 786440 | tf_op jit(solution)/shard_map/ppermute | solution.py:175
  54.2 2.6 %collective-permute-done.7 = bf16[256,512]{1,0:T(8,128)(2,1)S(1)} collective-permute-done((bf16[256,512]{1,0:T(8,128)(2,1)S(1)}, bf16[256,512]{1,0:T(8,128)(2,1)S(1)}, u32[]{:S(2)}, u32[]{:S(2)}) %collective-permute-start.7) | collective-permute-done | bytes 262176 | tf_op jit(solution)/shard_map/ppermute | solution.py:175
  56.7 0.0 copy-start.1
  56.7 3.8 %collective-permute-start.11 = (bf16[1280,512]{1,0:T(8,128)(2,1)S(1)}, bf16[1280,512]{1,0:T(8,128)(2,1)}, u32[]{:S(2)}, u32[]{:S(2)}) collective-permute-start(bf16[1280,512]{1,0:T(8,128)(2,1)S(1)} %constant_dynamic-update-slice_fusion.2), channel_id=1, source_target_pairs={{0,8},{8,0},{16,24},{24,16},{32,40},{40,32},{48,56},{56,48},{64,72... | collective-permute-start | bytes 3932168 | tf_op jit(solution)/shard_map/ppermute | solution.py:175
  60.6 5.3 %collective-permute-start.9 = (bf16[256,512]{1,0:T(8,128)(2,1)S(1)}, bf16[256,512]{1,0:T(8,128)(2,1)S(1)}, u32[]{:S(2)}, u32[]{:S(2)}) collective-permute-start(bf16[256,512]{1,0:T(8,128)(2,1)S(1)} %collective-permute-done.7), channel_id=1, source_target_pairs={{0,112},{8,120},{16,0},{24,8},{32,16},{40,24},{48,32},{56,40},{64,... | collective-permute-start | bytes 786440 | tf_op jit(solution)/shard_map/ppermute | solution.py:175
  65.9 0.0 collective-permute-done.8
  65.9 1.9 %collective-permute-start.10 = (bf16[256,512]{1,0:T(8,128)(2,1)S(1)}, bf16[256,512]{1,0:T(8,128)(2,1)S(1)}, u32[]{:S(2)}, u32[]{:S(2)}) collective-permute-start(bf16[256,512]{1,0:T(8,128)(2,1)S(1)} %collective-permute-done.8), channel_id=1, source_target_pairs={{0,16},{8,24},{16,32},{24,40},{32,48},{40,56},{48,64},{56,72},{64,... | collective-permute-start | bytes 786440 | tf_op jit(solution)/shard_map/ppermute | solution.py:175
  67.9 3.7 %collective-permute-done.9 = bf16[256,512]{1,0:T(8,128)(2,1)S(1)} collective-permute-done((bf16[256,512]{1,0:T(8,128)(2,1)S(1)}, bf16[256,512]{1,0:T(8,128)(2,1)S(1)}, u32[]{:S(2)}, u32[]{:S(2)}) %collective-permute-start.9) | collective-permute-done | bytes 262176 | tf_op jit(solution)/shard_map/ppermute | solution.py:175
  71.6 5.0 %collective-permute-done.10 = bf16[256,512]{1,0:T(8,128)(2,1)S(1)} collective-permute-done((bf16[256,512]{1,0:T(8,128)(2,1)S(1)}, bf16[256,512]{1,0:T(8,128)(2,1)S(1)}, u32[]{:S(2)}, u32[]{:S(2)}) %collective-permute-start.10) | collective-permute-done | bytes 262176 | tf_op jit(solution)/shard_map/ppermute | solution.py:175
  76.7 0.0 copy-start
  76.7 3.0 %collective-permute-start.12 = (bf16[768,512]{1,0:T(8,128)(2,1)S(1)}, bf16[768,512]{1,0:T(8,128)(2,1)S(1)}, u32[]{:S(2)}, u32[]{:S(2)}) collective-permute-start(bf16[768,512]{1,0:T(8,128)(2,1)S(1)} %constant_dynamic-update-slice_fusion.8), channel_id=1, source_target_pairs={{0,8},{8,0},{16,24},{24,16},{32,40},{40,32},{48,56},{56,48},{64,72... | collective-permute-start | bytes 2359304 | tf_op jit(solution)/shard_map/ppermute | solution.py:175
  79.7 0.7 pad_add_fusion.me_ref
  80.4 1.2 %collective-permute-done.12 = bf16[768,512]{1,0:T(8,128)(2,1)S(1)} collective-permute-done((bf16[768,512]{1,0:T(8,128)(2,1)S(1)}, bf16[768,512]{1,0:T(8,128)(2,1)S(1)}, u32[]{:S(2)}, u32[]{:S(2)}) %collective-permute-start.12) | collective-permute-done | bytes 786464 | tf_op jit(solution)/shard_map/ppermute | solution.py:175
  81.6 0.0 copy-start.2
  81.6 0.0 collective-permute-done.11
  81.6 0.0 all-gather.3.cloned.1.call-done
  81.6 0.0 copy-done.1
  81.6 0.0 copy-done
  81.6 0.9 copy-done.2
  82.6 10.5 %attend.1 = (bf16[512,512]{1,0:T(8,128)(2,1)}, bf16[512,128]{1,0:T(8,128)(2,1)}, bf16[512,128]{1,0:T(8,128)(2,1)}) custom-call(s32[3]{0:T(128)} %pad_add_fusion.me_ref, bf16[8,512,512]{2,1,0:T(8,128)(2,1)} %bitcast.16, bf16[5,4,64,512]{3,2,1,0:T(8,128)(2,1)} %bitcast.13, bf16[3,4,64,512]{3,2,1,0:T(8,128)(2,1)} %bitcast.12, ...), custom_call_target="tpu_custom_call" | custom-call | flops 4294967296 | bytes 12582912 | tf_op jit(solution)/shard_map/attend/pallas_call | solution.py:244
  (9 shorter events, 0.2 us)
Async XLA Ops:
  7.2 74.4 %all-gather.3.cloned.1.call-start = ((), (), s32[]{:S(2)}) async-start(), calls=%async_computation | async-start | bytes 4718592 | tf_op jit(solution)/shard_map/all_gather | solution.py:196
  7.9 6.5 %collective-permute-start = (bf16[64,512]{1,0:T(8,128)(2,1)}, bf16[64,512]{1,0:T(8,128)(2,1)S(1)}, u32[]{:S(2)}, u32[]{:S(2)}) collective-permute-start(bf16[64,512]{1,0:T(8,128)(2,1)} %param.15), channel_id=1, source_target_pairs={{0,128},{8,136},{16,144},{24,152},{32,160},{40,168},{48,176},{56,1... | collective-permute-start | bytes 196616 | tf_op jit(solution)/shard_map/ppermute | solution.py:175
  15.3 6.9 %collective-permute-start.1 = (bf16[128,512]{1,0:T(8,128)(2,1)S(1)}, bf16[128,512]{1,0:T(8,128)(2,1)S(1)}, u32[]{:S(2)}, u32[]{:S(2)}) collective-permute-start(bf16[128,512]{1,0:T(8,128)(2,1)S(1)} %pad_maximum_fusion), channel_id=1, source_target_pairs={{0,384},{8,392},{16,400},{24,408},{32,416},{40,424},{48,432},{56,4... | collective-permute-start | bytes 393224 | tf_op jit(solution)/shard_map/ppermute | solution.py:175
  22.2 19.2 %collective-permute-start.2 = (bf16[256,512]{1,0:T(8,128)(2,1)S(1)}, bf16[256,512]{1,0:T(8,128)(2,1)S(1)}, u32[]{:S(2)}, u32[]{:S(2)}) collective-permute-start(bf16[256,512]{1,0:T(8,128)(2,1)S(1)} %get-tuple-element.17), channel_id=1, source_target_pairs={{0,16},{8,24},{16,32},{24,40},{32,48},{40,56},{48,64},{56,72},{64,... | collective-permute-start | bytes 786440 | tf_op jit(solution)/shard_map/ppermute | solution.py:175
  26.2 21.3 %collective-permute-start.3 = (bf16[256,512]{1,0:T(8,128)(2,1)S(1)}, bf16[256,512]{1,0:T(8,128)(2,1)S(1)}, u32[]{:S(2)}, u32[]{:S(2)}) collective-permute-start(bf16[256,512]{1,0:T(8,128)(2,1)S(1)} %get-tuple-element.17), channel_id=1, source_target_pairs={{0,112},{8,120},{16,0},{24,8},{32,16},{40,24},{48,32},{56,40},{64,... | collective-permute-start | bytes 786440 | tf_op jit(solution)/shard_map/ppermute | solution.py:175
  34.8 8.6 %collective-permute-start.6 = (bf16[80,640]{1,0:T(8,128)(2,1)}, bf16[80,640]{1,0:T(8,128)(2,1)S(1)}, u32[]{:S(2)}, u32[]{:S(2)}) collective-permute-start(bf16[80,640]{1,0:T(8,128)(2,1)} %get-tuple-element.10), channel_id=1, source_target_pairs={{8,0},{16,8},{24,16},{32,24},{40,32},{48,40},{56,48},{64,56},{72,6... | collective-permute-start | bytes 307208 | tf_op jit(solution)/shard_map/ppermute | solution.py:219
  39.5 3.9 %collective-permute-start.5 = (bf16[80,640]{1,0:T(8,128)(2,1)}, bf16[80,640]{1,0:T(8,128)(2,1)S(1)}, u32[]{:S(2)}, u32[]{:S(2)}) collective-permute-start(bf16[80,640]{1,0:T(8,128)(2,1)} %get-tuple-element.11), channel_id=1, source_target_pairs={{0,8},{8,16},{16,24},{24,32},{32,40},{40,48},{48,56},{56,64},{64,7... | collective-permute-start | bytes 307208 | tf_op jit(solution)/shard_map/ppermute | solution.py:218
  41.5 10.7 %collective-permute-start.4 = (bf16[256,512]{1,0:T(8,128)(2,1)S(1)}, bf16[256,512]{1,0:T(8,128)(2,1)S(1)}, u32[]{:S(2)}, u32[]{:S(2)}) collective-permute-start(bf16[256,512]{1,0:T(8,128)(2,1)S(1)} %collective-permute-done.2), channel_id=1, source_target_pairs={{0,16},{8,24},{16,32},{24,40},{32,48},{40,56},{48,64},{56,72},{64,... | collective-permute-start | bytes 786440 | tf_op jit(solution)/shard_map/ppermute | solution.py:175
  43.4 0.6 copy-start.3
  43.4 0.7 copy-start.4
  47.6 9.2 %collective-permute-start.7 = (bf16[256,512]{1,0:T(8,128)(2,1)S(1)}, bf16[256,512]{1,0:T(8,128)(2,1)S(1)}, u32[]{:S(2)}, u32[]{:S(2)}) collective-permute-start(bf16[256,512]{1,0:T(8,128)(2,1)S(1)} %collective-permute-done.3), channel_id=1, source_target_pairs={{0,112},{8,120},{16,0},{24,8},{32,16},{40,24},{48,32},{56,40},{64,... | collective-permute-start | bytes 786440 | tf_op jit(solution)/shard_map/ppermute | solution.py:175
  52.2 13.7 %collective-permute-start.8 = (bf16[256,512]{1,0:T(8,128)(2,1)S(1)}, bf16[256,512]{1,0:T(8,128)(2,1)S(1)}, u32[]{:S(2)}, u32[]{:S(2)}) collective-permute-start(bf16[256,512]{1,0:T(8,128)(2,1)S(1)} %collective-permute-done.4), channel_id=1, source_target_pairs={{0,16},{8,24},{16,32},{24,40},{32,48},{40,56},{48,64},{56,72},{64,... | collective-permute-start | bytes 786440 | tf_op jit(solution)/shard_map/ppermute | solution.py:175
  56.7 24.9 %copy-start.1 = (bf16[1280,512]{1,0:T(8,128)(2,1)}, bf16[1280,512]{1,0:T(8,128)(2,1)S(1)}, u32[]{:S(2)}) copy-start(bf16[1280,512]{1,0:T(8,128)(2,1)S(1)} %constant_dynamic-update-slice_fusion.2) | copy-start | bytes 3932164
  56.7 24.8 %collective-permute-start.11 = (bf16[1280,512]{1,0:T(8,128)(2,1)S(1)}, bf16[1280,512]{1,0:T(8,128)(2,1)}, u32[]{:S(2)}, u32[]{:S(2)}) collective-permute-start(bf16[1280,512]{1,0:T(8,128)(2,1)S(1)} %constant_dynamic-update-slice_fusion.2), channel_id=1, source_target_pairs={{0,8},{8,0},{16,24},{24,16},{32,40},{40,32},{48,56},{56,48},{64,72... | collective-permute-start | bytes 3932168 | tf_op jit(solution)/shard_map/ppermute | solution.py:175
  60.6 11.0 %collective-permute-start.9 = (bf16[256,512]{1,0:T(8,128)(2,1)S(1)}, bf16[256,512]{1,0:T(8,128)(2,1)S(1)}, u32[]{:S(2)}, u32[]{:S(2)}) collective-permute-start(bf16[256,512]{1,0:T(8,128)(2,1)S(1)} %collective-permute-done.7), channel_id=1, source_target_pairs={{0,112},{8,120},{16,0},{24,8},{32,16},{40,24},{48,32},{56,40},{64,... | collective-permute-start | bytes 786440 | tf_op jit(solution)/shard_map/ppermute | solution.py:175
  65.9 10.7 %collective-permute-start.10 = (bf16[256,512]{1,0:T(8,128)(2,1)S(1)}, bf16[256,512]{1,0:T(8,128)(2,1)S(1)}, u32[]{:S(2)}, u32[]{:S(2)}) collective-permute-start(bf16[256,512]{1,0:T(8,128)(2,1)S(1)} %collective-permute-done.8), channel_id=1, source_target_pairs={{0,16},{8,24},{16,32},{24,40},{32,48},{40,56},{48,64},{56,72},{64,... | collective-permute-start | bytes 786440 | tf_op jit(solution)/shard_map/ppermute | solution.py:175
  76.7 4.9 %copy-start = (bf16[768,512]{1,0:T(8,128)(2,1)}, bf16[768,512]{1,0:T(8,128)(2,1)S(1)}, u32[]{:S(2)}) copy-start(bf16[768,512]{1,0:T(8,128)(2,1)S(1)} %constant_dynamic-update-slice_fusion.8) | copy-start | bytes 2359300
  76.7 4.9 %collective-permute-start.12 = (bf16[768,512]{1,0:T(8,128)(2,1)S(1)}, bf16[768,512]{1,0:T(8,128)(2,1)S(1)}, u32[]{:S(2)}, u32[]{:S(2)}) collective-permute-start(bf16[768,512]{1,0:T(8,128)(2,1)S(1)} %constant_dynamic-update-slice_fusion.8), channel_id=1, source_target_pairs={{0,8},{8,0},{16,24},{24,16},{32,40},{40,32},{48,56},{56,48},{64,72... | collective-permute-start | bytes 2359304 | tf_op jit(solution)/shard_map/ppermute | solution.py:175
  81.6 1.0 copy-start.2
Sparse Core Ops, SparseCore 0:
  10.1 62.6 all-gather.2

commit v2 on v1

--- a/solution.py
+++ b/solution.py
@@ -95,20 +95,28 @@
     ]
     for copy in ins:
         copy.start()
-    for refs, core in (((near_ref, far_ref), my_core), ((near_other_ref, far_other_ref), 1 - my_core)):
-        for piece_ref, z_steps in zip(refs, (NEAR, FAR)):
-            for index, step in enumerate(z_steps):
-                z = lax.rem(my_z + step + Z, Z)
-                pltpu.make_async_copy(
-                    piece_ref.at[index], weight_buf.at[z, :, core], weight_sems.at[2 * z + core]
-                ).start()
-    grads = []
-    for half in range(2):
-        for index, step in enumerate(COLUMN):
-            part = 2 * (my_x ^ step) + half
-            copy = pltpu.make_async_copy(grad_ref.at[part], grad_buf.at[index, half], grad_sems.at[index, half])
-            copy.start()
-            grads.append(copy)
+    batches = []
+    for batch in range(2):
+        own = slice(batch * X // 2, (batch + 1) * X // 2)
+        copies = []
+        for refs, core in (((near_ref, far_ref), my_core), ((near_other_ref, far_other_ref), 1 - my_core)):
+            for piece_ref, z_steps in zip(refs, (NEAR, FAR)):
+                for index, step in enumerate(z_steps):
+                    z = lax.rem(my_z + step + Z, Z)
+                    copies.append(
+                        pltpu.make_async_copy(
+                            piece_ref.at[index, own], weight_buf.at[z, own, core], weight_sems.at[batch, len(copies)]
+                        )
+                    )
+        for index in range(own.start, own.stop):
+            for half in range(2):
+                part = 2 * (my_x ^ COLUMN[index]) + half
+                copies.append(
+                    pltpu.make_async_copy(grad_ref.at[part], grad_buf.at[index, half], grad_sems.at[index, half])
+                )
+        batches.append(copies)
+    for copy in batches[0]:
+        copy.start()
     for copy in ins[:3]:
         copy.wait()
     for i, j in tiles_of(rows):
@@ -120,22 +128,22 @@
         for h in range(GROUP):
             score = dot(key_ref[others, :], query_ref[tokens, h * HD : (h + 1) * HD], NT) * scale
             prob[h, others, tokens] = jnp.where(allowed, jnp.exp(score - stats_ref[h : h + 1, tokens]), 0.0)
-    for z in range(Z):
-        half, place = z // (Z // 2), z % (Z // 2)
-        for core in range(2):
-            pltpu.make_async_copy(near_ref.at[0], weight_buf.at[z, :, core], weight_sems.at[2 * z + core]).wait()
-        if place == 0:
-            for copy in grads[half * X : (half + 1) * X]:
-                copy.wait()
-        left = jnp.concatenate([grad_buf[x, half, :, place * 128 : (place + 1) * 128] for x in range(X)], axis=1)
-        product = dot(left, weight_buf[z].reshape(depth, -1))
-        if z == 0:
+    for copy in batches[1]:
+        copy.start()
+    for batch, copies in enumerate(batches):
+        for copy in copies:
+            copy.wait()
+        product = 0.0
+        for index in range(batch * X // 2, (batch + 1) * X // 2):
+            for half in range(2):
+                right = weight_buf[half * (Z // 2) : (half + 1) * (Z // 2), index].reshape(depth, -1)
+                product += dot(grad_buf[index, half], right)
+        if batch == 0:
             total[...] = product
         else:
-            total[...] += product
+            heads[...] = (total[...] + product).astype(jnp.bfloat16)
     for copy in ins[3:]:
         copy.wait()
-    heads[...] = total[...].astype(jnp.bfloat16)
     delta = jnp.zeros((rows, HD), jnp.float32)
     for h in range(GROUP):
         cols = slice(h * HD, (h + 1) * HD)
@@ -188,6 +196,39 @@
 NEAR, FAR = (0, -1, 1, -2, 2), (-3, 3, 4)
 
 
+def attend(place, all_grad, near, far, near_other, far_other, queries, keys, values, attn, stats):
+    parts, rows, depth = all_grad.shape
+    width, key_width = queries.shape[1], keys.shape[1]
+    return pl.pallas_call(
+        attend_kernel,
+        out_shape=(
+            jax.ShapeDtypeStruct((rows, width), jnp.bfloat16),
+            jax.ShapeDtypeStruct((rows, key_width), jnp.bfloat16),
+            jax.ShapeDtypeStruct((rows, key_width), jnp.bfloat16),
+        ),
+        in_specs=[SMEM] + [HBM] * 10,
+        out_specs=(VMEM, VMEM, VMEM),
+        scratch_shapes=[
+            pltpu.VMEM((X, 2, rows, depth), jnp.bfloat16),
+            pltpu.VMEM((Z, X, 2, *near.shape[2:]), jnp.bfloat16),
+            pltpu.VMEM(queries.shape, jnp.bfloat16),
+            pltpu.VMEM(keys.shape, jnp.bfloat16),
+            pltpu.VMEM(values.shape, jnp.bfloat16),
+            pltpu.VMEM(attn.shape, jnp.bfloat16),
+            pltpu.VMEM(stats.shape, jnp.float32),
+            pltpu.VMEM((rows, width), jnp.float32),
+            pltpu.VMEM((GROUP, rows, rows), jnp.float32),
+            pltpu.VMEM((rows, width), jnp.bfloat16),
+            pltpu.SemaphoreType.DMA((X, 2)),
+            pltpu.SemaphoreType.DMA((2, 2 * Z)),
+            pltpu.SemaphoreType.DMA((5,)),
+        ],
+        compiler_params=pltpu.CompilerParams(vmem_limit_bytes=60 << 20),
+        cost_estimate=pl.CostEstimate(flops=4 << 30, bytes_accessed=12 << 20, transcendentals=1 << 20),
+        name="attend",
+    )(place, all_grad, near, far, near_other, far_other, queries, keys, values, attn, stats)
+
+
 def on_device(
     queries, keys, values, attn_out, grad_out, out_weight, log_norm, source_row, dest_row, slot_start
 ):
@@ -213,12 +254,19 @@
     down = lambda x, z, c: (x, z - 1, c)
     other = lambda x, z, c: (x, z, 1 - c)
     pair = jnp.concatenate([out_weight, move(out_weight, lambda x, z, c: (x ^ 1, z, c))], axis=0)
-    pair = after(pair, to_low, to_high)
+    column = jnp.concatenate([pair, move(pair, lambda x, z, c: (3 - x, z, c))], axis=0)
+    column = after(column, to_low, to_high)
+    up1, down1 = move(column, up), move(column, down)
+    up2, down2 = move(up1, up), move(down1, down)
+    up3 = move(up2, up)
+    near = jnp.concatenate([column, up1, down1, up2, down2], axis=0)
+    near_other = move(near, other)
+    down3 = move(down2, down)
+    up4 = move(up3, up)
+    to_low, to_high = lax.optimization_barrier((to_low, to_high, down3))[:2]
     forward = [(i, i + 1) for i in range(lax.axis_size("dp") - 1)]
     from_low = lax.ppermute(to_high, "dp", forward)
     from_high = lax.ppermute(to_low, "dp", [(b, a) for a, b in forward])
-    column = jnp.concatenate([pair, move(pair, lambda x, z, c: (3 - x, z, c))], axis=0)
-    up1 = move(column, up)
     attn_packed, stats_packed = pl.pallas_call(
         receive_kernel,
         out_shape=(
@@ -230,45 +278,11 @@
         cost_estimate=pl.CostEstimate(flops=2 * rows * rows * 640, bytes_accessed=2 << 20, transcendentals=0),
         name="receive_rows",
     )(first, dest_row[None], attn_out, stats, from_low, from_high)
-    down1 = move(column, down)
-    up2, down2 = move(up1, up), move(after(down1, attn_packed, stats_packed), down)
-    up3, down3 = move(up2, up), move(down2, down)
-    up4 = move(up3, up)
-    near = jnp.concatenate([column, up1, down1, up2, down2], axis=0)
-    near_other = move(near, other)
-    far = jnp.concatenate([up3, down3, up4], axis=0)
+    far = jnp.concatenate([up3, after(down3, attn_packed, stats_packed), up4], axis=0)
     far_other = move(far, other)
     pieces = [piece.reshape(-1, X, *out_weight.shape) for piece in (near, far, near_other, far_other)]
 
-    parts, _, depth = all_grad.shape
-    return pl.pallas_call(
-        attend_kernel,
-        out_shape=(
-            jax.ShapeDtypeStruct((rows, width), jnp.bfloat16),
-            jax.ShapeDtypeStruct((rows, key_width), jnp.bfloat16),
-            jax.ShapeDtypeStruct((rows, key_width), jnp.bfloat16),
-        ),
-        in_specs=[SMEM] + [HBM] * 10,
-        out_specs=(VMEM, VMEM, VMEM),
-        scratch_shapes=[
-            pltpu.VMEM((X, 2, rows, depth), jnp.bfloat16),
-            pltpu.VMEM((Z, X, 2, *out_weight.shape), jnp.bfloat16),
-            pltpu.VMEM(queries.shape, jnp.bfloat16),
-            pltpu.VMEM(keys.shape, jnp.bfloat16),
-            pltpu.VMEM(values.shape, jnp.bfloat16),
-            pltpu.VMEM(attn_out.shape, jnp.bfloat16),
-            pltpu.VMEM(stats_packed.shape, jnp.float32),
-            pltpu.VMEM((rows, width), jnp.float32),
-            pltpu.VMEM((GROUP, rows, rows), jnp.float32),
-            pltpu.VMEM((rows, width), jnp.bfloat16),
-            pltpu.SemaphoreType.DMA((X, 2)),
-            pltpu.SemaphoreType.DMA((2 * Z,)),
-            pltpu.SemaphoreType.DMA((5,)),
-        ],
-        compiler_params=pltpu.CompilerParams(vmem_limit_bytes=60 << 20),
-        cost_estimate=pl.CostEstimate(flops=4 << 30, bytes_accessed=12 << 20, transcendentals=1 << 20),
-        name="attend",
-    )(place, all_grad, *pieces, queries, keys, values, attn_packed, stats_packed)
+    return attend(place, all_grad, *pieces, queries, keys, values, attn_packed, stats_packed)
 
 
 def solution(mesh):

time: 101 us -> 97.3 us (0.963)
  waiting for transfers between devices: 16.2 us -> 10.1 us
  starting transfers between devices: 49.6 us -> 53 us
    ppermute x11, waiting for transfers between devices: 15.5 us -> 7.46 us  [move(): return lax.ppermute(block, 'dp', pairs)]
    ppermute x11, starting transfers between devices: 43 us -> 48.7 us  [move(): return lax.ppermute(block, 'dp', pairs)]
    ppermute x1, starting transfers between devices: 4.69 us -> 2.41 us  [on_device(): from_high = lax.ppermute(to_low, 'dp', [(b, a) for a, b in forward])]
    ppermute x1, waiting for transfers between devices: 0.01 us -> 1.98 us  [on_device(): from_high = lax.ppermute(to_low, 'dp', [(b, a) for a, b in forward])]
  transfers between devices with their start and end apart: 14 -> 14, of which waited for: 5 -> 6; matrix products, arithmetic and copies ran while one was open for 2% -> 2% of each run, Pallas kernels for 6% -> 6%
where the time goes in v2:
time: 97.3 us; the launch traced here: 96.7 us
  starting transfers between devices  53 us (54%)
  Pallas kernels  15.9 us (16%)
  between operations  14.4 us (15%)
  waiting for transfers between devices  10.1 us (10%)
  local copies, waits for them, and re-layouts  1.79 us (2%)
  other arithmetic  1.52 us (2%)
    ppermute x11, starting transfers between devices, move(): return lax.ppermute(block, 'dp', pairs)  48.7 us
    pallas_call x1, Pallas kernels, attend(): pl.pallas_call(attend_kernel, out_shape=(jax.ShapeDtypeStruct((rows, widt...  9.84 us
    ppermute x11, waiting for transfers between devices, move(): return lax.ppermute(block, 'dp', pairs)  7.46 us
    pallas_call x1, Pallas kernels, on_device(): pl.pallas_call(receive_kernel, out_shape=(jax.ShapeDtypeStruct((rows, wid...  3.48 us
    pallas_call x1, Pallas kernels, on_device(): pl.pallas_call(send_kernel, out_shape=(message, message, jax.ShapeDtypeSt...  2.56 us
    ppermute x1, starting transfers between devices, on_device(): from_high = lax.ppermute(to_low, 'dp', [(b, a) for a, b in forward])  2.41 us
    ppermute x1, waiting for transfers between devices, on_device(): from_high = lax.ppermute(to_low, 'dp', [(b, a) for a, b in forward])  1.98 us
  transfers between devices with their start and end apart: 14, of which 6 were waited for; matrix products, arithmetic and copies ran while one was open for 2% of the time, Pallas kernels for 6%

profile of v2, /device:TPU:1, one launch (start us, length us, event | category | flops | bytes accessed | tf_op | source)
XLA Modules:
  0.0 96.7 jit_solution(14125312330333475304)
XLA Ops:
  7.2 0.0 copy-start
  7.2 0.0 all-gather.3.cloned.1.call-start
  7.2 0.7 all-gather.3.cloned.1.call-update
  7.9 3.9 %collective-permute-start = (bf16[64,512]{1,0:T(8,128)(2,1)}, bf16[64,512]{1,0:T(8,128)(2,1)S(1)}, u32[]{:S(2)}, u32[]{:S(2)}) collective-permute-start(bf16[64,512]{1,0:T(8,128)(2,1)} %param.15), channel_id=1, source_target_pairs={{0,128},{8,136},{16,144},{24,152},{32,160},{40,168},{48,176},{56,1... | collective-permute-start | bytes 196616 | tf_op jit(solution)/shard_map/ppermute | solution.py:183
  11.9 1.9 %collective-permute-done = bf16[64,512]{1,0:T(8,128)(2,1)S(1)} collective-permute-done((bf16[64,512]{1,0:T(8,128)(2,1)}, bf16[64,512]{1,0:T(8,128)(2,1)S(1)}, u32[]{:S(2)}, u32[]{:S(2)}) %collective-permute-start) | collective-permute-done | bytes 65568 | tf_op jit(solution)/shard_map/ppermute | solution.py:183
  13.7 0.8 pad_maximum_fusion.1
  14.6 4.6 %collective-permute-start.1 = (bf16[128,512]{1,0:T(8,128)(2,1)S(1)}, bf16[128,512]{1,0:T(8,128)(2,1)S(1)}, u32[]{:S(2)}, u32[]{:S(2)}) collective-permute-start(bf16[128,512]{1,0:T(8,128)(2,1)S(1)} %pad_maximum_fusion.1), channel_id=1, source_target_pairs={{0,384},{8,392},{16,400},{24,408},{32,416},{40,424},{48,432},{56,4... | collective-permute-start | bytes 393224 | tf_op jit(solution)/shard_map/ppermute | solution.py:183
  19.2 2.6 %send_rows.1 = (bf16[80,640]{1,0:T(8,128)(2,1)}, bf16[80,640]{1,0:T(8,128)(2,1)}, bf16[128,512]{1,0:T(8,128)(2,1)}) custom-call(s32[1]{0:T(128)} %bitcast.4.first_ref, s32[1,512]{1,0:T(1,128)} %bitcast.14, s32[1,512]{1,0:T(1,128)} %bitcast.15, f32[4,512]{1,0:T(4,128)} %norm_ref.1, bf16[512,512]{1,0:T(8,128)(2,1)} %attn_ref.3), custom_call_target="tpu_custom_call" | custom-call | flops 104857600 | bytes 1048576 | tf_op jit(solution)/shard_map/send_rows/pallas_call | solution.py:243
  21.8 0.0 collective-permute-done.1
  21.8 0.0 copy-done
  21.8 0.0 copy-start.5
  21.8 0.0 copy-start.4
  21.8 10.8 %collective-permute-start.3 = (bf16[256,512]{1,0:T(8,128)(2,1)S(1)}, bf16[256,512]{1,0:T(8,128)(2,1)S(1)}, u32[]{:S(2)}, u32[]{:S(2)}) collective-permute-start(bf16[256,512]{1,0:T(8,128)(2,1)S(1)} %pad_maximum_fusion), channel_id=1, source_target_pairs={{0,112},{8,120},{16,0},{24,8},{32,16},{40,24},{48,32},{56,40},{64,... | collective-permute-start | bytes 786440 | tf_op jit(solution)/shard_map/ppermute | solution.py:183
  32.6 1.9 %collective-permute-start.2 = (bf16[256,512]{1,0:T(8,128)(2,1)S(1)}, bf16[256,512]{1,0:T(8,128)(2,1)S(1)}, u32[]{:S(2)}, u32[]{:S(2)}) collective-permute-start(bf16[256,512]{1,0:T(8,128)(2,1)S(1)} %pad_maximum_fusion), channel_id=1, source_target_pairs={{0,16},{8,24},{16,32},{24,40},{32,48},{40,56},{48,64},{56,72},{64,... | collective-permute-start | bytes 786440 | tf_op jit(solution)/shard_map/ppermute | solution.py:183
  34.6 1.4 %collective-permute-done.3 = bf16[256,512]{1,0:T(8,128)(2,1)S(1)} collective-permute-done((bf16[256,512]{1,0:T(8,128)(2,1)S(1)}, bf16[256,512]{1,0:T(8,128)(2,1)S(1)}, u32[]{:S(2)}, u32[]{:S(2)}) %collective-permute-start.3) | collective-permute-done | bytes 262176 | tf_op jit(solution)/shard_map/ppermute | solution.py:183
  35.9 5.4 %collective-permute-start.5 = (bf16[256,512]{1,0:T(8,128)(2,1)S(1)}, bf16[256,512]{1,0:T(8,128)(2,1)S(1)}, u32[]{:S(2)}, u32[]{:S(2)}) collective-permute-start(bf16[256,512]{1,0:T(8,128)(2,1)S(1)} %collective-permute-done.3), channel_id=1, source_target_pairs={{0,112},{8,120},{16,0},{24,8},{32,16},{40,24},{48,32},{56,40},{64,... | collective-permute-start | bytes 786440 | tf_op jit(solution)/shard_map/ppermute | solution.py:183
  41.3 0.0 collective-permute-done.2
  41.4 1.9 %collective-permute-start.4 = (bf16[256,512]{1,0:T(8,128)(2,1)S(1)}, bf16[256,512]{1,0:T(8,128)(2,1)S(1)}, u32[]{:S(2)}, u32[]{:S(2)}) collective-permute-start(bf16[256,512]{1,0:T(8,128)(2,1)S(1)} %collective-permute-done.2), channel_id=1, source_target_pairs={{0,16},{8,24},{16,32},{24,40},{32,48},{40,56},{48,64},{56,72},{64,... | collective-permute-start | bytes 786440 | tf_op jit(solution)/shard_map/ppermute | solution.py:183
  43.4 1.3 %collective-permute-done.5 = bf16[256,512]{1,0:T(8,128)(2,1)S(1)} collective-permute-done((bf16[256,512]{1,0:T(8,128)(2,1)S(1)}, bf16[256,512]{1,0:T(8,128)(2,1)S(1)}, u32[]{:S(2)}, u32[]{:S(2)}) %collective-permute-start.5) | collective-permute-done | bytes 262176 | tf_op jit(solution)/shard_map/ppermute | solution.py:183
  44.6 5.4 %collective-permute-start.7 = (bf16[256,512]{1,0:T(8,128)(2,1)S(1)}, bf16[256,512]{1,0:T(8,128)(2,1)S(1)}, u32[]{:S(2)}, u32[]{:S(2)}) collective-permute-start(bf16[256,512]{1,0:T(8,128)(2,1)S(1)} %collective-permute-done.5), channel_id=1, source_target_pairs={{0,112},{8,120},{16,0},{24,8},{32,16},{40,24},{48,32},{56,40},{64,... | collective-permute-start | bytes 786440 | tf_op jit(solution)/shard_map/ppermute | solution.py:183
  50.1 0.0 collective-permute-done.4
  50.1 1.9 %collective-permute-start.6 = (bf16[256,512]{1,0:T(8,128)(2,1)S(1)}, bf16[256,512]{1,0:T(8,128)(2,1)S(1)}, u32[]{:S(2)}, u32[]{:S(2)}) collective-permute-start(bf16[256,512]{1,0:T(8,128)(2,1)S(1)} %collective-permute-done.4), channel_id=1, source_target_pairs={{0,16},{8,24},{16,32},{24,40},{32,48},{40,56},{48,64},{56,72},{64,... | collective-permute-start | bytes 786440 | tf_op jit(solution)/shard_map/ppermute | solution.py:183
  52.1 0.0 copy-start.2
  52.1 6.6 %collective-permute-start.11 = (bf16[1280,512]{1,0:T(8,128)(2,1)S(1)}, bf16[1280,512]{1,0:T(8,128)(2,1)}, u32[]{:S(2)}, u32[]{:S(2)}) collective-permute-start(bf16[1280,512]{1,0:T(8,128)(2,1)S(1)} %constant_dynamic-update-slice_fusion), channel_id=1, source_target_pairs={{0,8},{8,0},{16,24},{24,16},{32,40},{40,32},{48,56},{56,48},{64,72... | collective-permute-start | bytes 3932168 | tf_op jit(solution)/shard_map/ppermute | solution.py:183
  58.7 0.0 collective-permute-done.7
  58.7 0.0 copy-done.5
  58.7 1.9 %collective-permute-start.8 = (bf16[80,640]{1,0:T(8,128)(2,1)S(1)}, bf16[80,640]{1,0:T(8,128)(2,1)S(1)}, u32[]{:S(2)}, u32[]{:S(2)}) collective-permute-start(bf16[80,640]{1,0:T(8,128)(2,1)S(1)} %copy-done.5), channel_id=1, source_target_pairs={{0,8},{8,16},{16,24},{24,32},{32,40},{40,48},{48,56},{56,64},{64,7... | collective-permute-start | bytes 307208 | tf_op jit(solution)/shard_map/ppermute | solution.py:268
  60.6 0.0 copy-done.4
  60.7 2.4 %collective-permute-start.9 = (bf16[80,640]{1,0:T(8,128)(2,1)S(1)}, bf16[80,640]{1,0:T(8,128)(2,1)S(1)}, u32[]{:S(2)}, u32[]{:S(2)}) collective-permute-start(bf16[80,640]{1,0:T(8,128)(2,1)S(1)} %copy-done.4), channel_id=1, source_target_pairs={{8,0},{16,8},{24,16},{32,24},{40,32},{48,40},{56,48},{64,56},{72,6... | collective-permute-start | bytes 307208 | tf_op jit(solution)/shard_map/ppermute | solution.py:269
  63.1 0.0 collective-permute-done.6
  63.1 1.9 %collective-permute-start.10 = (bf16[256,512]{1,0:T(8,128)(2,1)S(1)}, bf16[256,512]{1,0:T(8,128)(2,1)S(1)}, u32[]{:S(2)}, u32[]{:S(2)}) collective-permute-start(bf16[256,512]{1,0:T(8,128)(2,1)S(1)} %collective-permute-done.6), channel_id=1, source_target_pairs={{0,16},{8,24},{16,32},{24,40},{32,48},{40,56},{48,64},{56,72},{64,... | collective-permute-start | bytes 786440 | tf_op jit(solution)/shard_map/ppermute | solution.py:183
  65.0 0.0 collective-permute-done.8.low_ref
  65.0 0.0 copy-start.6
  65.1 2.0 %collective-permute-done.9.high_ref = bf16[80,640]{1,0:T(8,128)(2,1)S(1)} collective-permute-done((bf16[80,640]{1,0:T(8,128)(2,1)S(1)}, bf16[80,640]{1,0:T(8,128)(2,1)S(1)}, u32[]{:S(2)}, u32[]{:S(2)}) %collective-permute-start.9) | collective-permute-done | bytes 102432 | tf_op jit(solution)/shard_map/ppermute | solution.py:269
  67.0 0.0 copy-start.7
  67.0 0.0 copy-done.6
  67.0 0.6 copy-done.7
  67.7 3.5 %receive_rows.1 = (bf16[512,512]{1,0:T(8,128)(2,1)}, f32[16,512]{1,0:T(8,128)}) custom-call(s32[1]{0:T(128)} %bitcast.4.first_ref, s32[1,512]{1,0:T(1,128)} %bitcast.18, bf16[512,512]{1,0:T(8,128)(2,1)} %attn_ref.3, bf16[128,512]{1,0:T(8,128)(2,1)} %get-tuple-element.15.stats_ref, bf16[80,640]{1,0:T(8,128)(2,1)} %copy-done.6, bf16[80,640]{1,0:T(8,128)(2,1)} %copy-done.7), custom_call_target="tpu_custom_call" | custom-call | flops 335544320 | bytes 2097152 | tf_op jit(solution)/shard_map/receive_rows/pallas_call | solution.py:270
  71.2 1.7 %collective-permute-done.10 = bf16[256,512]{1,0:T(8,128)(2,1)S(1)} collective-permute-done((bf16[256,512]{1,0:T(8,128)(2,1)S(1)}, bf16[256,512]{1,0:T(8,128)(2,1)S(1)}, u32[]{:S(2)}, u32[]{:S(2)}) %collective-permute-start.10) | collective-permute-done | bytes 262176 | tf_op jit(solution)/shard_map/ppermute | solution.py:183
  72.9 0.0 copy-done.2
  73.0 0.0 copy-start.1
  73.0 4.2 %collective-permute-start.12 = (bf16[768,512]{1,0:T(8,128)(2,1)S(1)}, bf16[768,512]{1,0:T(8,128)(2,1)S(1)}, u32[]{:S(2)}, u32[]{:S(2)}) collective-permute-start(bf16[768,512]{1,0:T(8,128)(2,1)S(1)} %constant_dynamic-update-slice_fusion.5), channel_id=1, source_target_pairs={{0,8},{8,0},{16,24},{24,16},{32,40},{40,32},{48,56},{56,48},{64,72... | collective-permute-start | bytes 2359304 | tf_op jit(solution)/shard_map/ppermute | solution.py:183
  77.2 0.7 pad_add_fusion.me_ref
  77.8 1.2 %collective-permute-done.12 = bf16[768,512]{1,0:T(8,128)(2,1)S(1)} collective-permute-done((bf16[768,512]{1,0:T(8,128)(2,1)S(1)}, bf16[768,512]{1,0:T(8,128)(2,1)S(1)}, u32[]{:S(2)}, u32[]{:S(2)}) %collective-permute-start.12) | collective-permute-done | bytes 786464 | tf_op jit(solution)/shard_map/ppermute | solution.py:183
  79.0 0.0 collective-permute-done.11
  79.0 0.0 copy-done.1
  79.0 1.0 copy-done.3
  80.0 9.8 %attend.1 = (bf16[512,512]{1,0:T(8,128)(2,1)}, bf16[512,128]{1,0:T(8,128)(2,1)}, bf16[512,128]{1,0:T(8,128)(2,1)}) custom-call(s32[3]{0:T(128)} %pad_add_fusion.me_ref, bf16[8,512,512]{2,1,0:T(8,128)(2,1)} %bitcast.16, bf16[5,4,64,512]{3,2,1,0:T(8,128)(2,1)} %bitcast.13, bf16[3,4,64,512]{3,2,1,0:T(8,128)(2,1)} %bitcast.12, ...), custom_call_target="tpu_custom_call" | custom-call | flops 4294967296 | bytes 12582912 | tf_op jit(solution)/shard_map/attend/pallas_call | solution.py:202
  (11 shorter events, 0.2 us)
Async XLA Ops:
  7.2 14.6 %copy-start = (bf16[64,512]{1,0:T(8,128)(2,1)S(1)}, bf16[64,512]{1,0:T(8,128)(2,1)}, u32[]{:S(2)}) copy-start(bf16[64,512]{1,0:T(8,128)(2,1)} %param.15) | copy-start | bytes 196612
  7.2 71.9 %all-gather.3.cloned.1.call-start = ((), (), s32[]{:S(2)}) async-start(), calls=%async_computation | async-start | bytes 4718592 | tf_op jit(solution)/shard_map/all_gather | solution.py:237
  7.9 5.8 %collective-permute-start = (bf16[64,512]{1,0:T(8,128)(2,1)}, bf16[64,512]{1,0:T(8,128)(2,1)S(1)}, u32[]{:S(2)}, u32[]{:S(2)}) collective-permute-start(bf16[64,512]{1,0:T(8,128)(2,1)} %param.15), channel_id=1, source_target_pairs={{0,128},{8,136},{16,144},{24,152},{32,160},{40,168},{48,176},{56,1... | collective-permute-start | bytes 196616 | tf_op jit(solution)/shard_map/ppermute | solution.py:183
  14.6 7.2 %collective-permute-start.1 = (bf16[128,512]{1,0:T(8,128)(2,1)S(1)}, bf16[128,512]{1,0:T(8,128)(2,1)S(1)}, u32[]{:S(2)}, u32[]{:S(2)}) collective-permute-start(bf16[128,512]{1,0:T(8,128)(2,1)S(1)} %pad_maximum_fusion.1), channel_id=1, source_target_pairs={{0,384},{8,392},{16,400},{24,408},{32,416},{40,424},{48,432},{56,4... | collective-permute-start | bytes 393224 | tf_op jit(solution)/shard_map/ppermute | solution.py:183
  21.8 36.9 %copy-start.5 = (bf16[80,640]{1,0:T(8,128)(2,1)S(1)}, bf16[80,640]{1,0:T(8,128)(2,1)}, u32[]{:S(2)}) copy-start(bf16[80,640]{1,0:T(8,128)(2,1)} %get-tuple-element.16) | copy-start | bytes 307204
  21.8 38.8 %copy-start.4 = (bf16[80,640]{1,0:T(8,128)(2,1)S(1)}, bf16[80,640]{1,0:T(8,128)(2,1)}, u32[]{:S(2)}) copy-start(bf16[80,640]{1,0:T(8,128)(2,1)} %get-tuple-element.17) | copy-start | bytes 307204
  21.8 14.1 %collective-permute-start.3 = (bf16[256,512]{1,0:T(8,128)(2,1)S(1)}, bf16[256,512]{1,0:T(8,128)(2,1)S(1)}, u32[]{:S(2)}, u32[]{:S(2)}) collective-permute-start(bf16[256,512]{1,0:T(8,128)(2,1)S(1)} %pad_maximum_fusion), channel_id=1, source_target_pairs={{0,112},{8,120},{16,0},{24,8},{32,16},{40,24},{48,32},{56,40},{64,... | collective-permute-start | bytes 786440 | tf_op jit(solution)/shard_map/ppermute | solution.py:183
  32.6 8.7 %collective-permute-start.2 = (bf16[256,512]{1,0:T(8,128)(2,1)S(1)}, bf16[256,512]{1,0:T(8,128)(2,1)S(1)}, u32[]{:S(2)}, u32[]{:S(2)}) collective-permute-start(bf16[256,512]{1,0:T(8,128)(2,1)S(1)} %pad_maximum_fusion), channel_id=1, source_target_pairs={{0,16},{8,24},{16,32},{24,40},{32,48},{40,56},{48,64},{56,72},{64,... | collective-permute-start | bytes 786440 | tf_op jit(solution)/shard_map/ppermute | solution.py:183
  35.9 8.7 %collective-permute-start.5 = (bf16[256,512]{1,0:T(8,128)(2,1)S(1)}, bf16[256,512]{1,0:T(8,128)(2,1)S(1)}, u32[]{:S(2)}, u32[]{:S(2)}) collective-permute-start(bf16[256,512]{1,0:T(8,128)(2,1)S(1)} %collective-permute-done.3), channel_id=1, source_target_pairs={{0,112},{8,120},{16,0},{24,8},{32,16},{40,24},{48,32},{56,40},{64,... | collective-permute-start | bytes 786440 | tf_op jit(solution)/shard_map/ppermute | solution.py:183
  41.4 8.7 %collective-permute-start.4 = (bf16[256,512]{1,0:T(8,128)(2,1)S(1)}, bf16[256,512]{1,0:T(8,128)(2,1)S(1)}, u32[]{:S(2)}, u32[]{:S(2)}) collective-permute-start(bf16[256,512]{1,0:T(8,128)(2,1)S(1)} %collective-permute-done.2), channel_id=1, source_target_pairs={{0,16},{8,24},{16,32},{24,40},{32,48},{40,56},{48,64},{56,72},{64,... | collective-permute-start | bytes 786440 | tf_op jit(solution)/shard_map/ppermute | solution.py:183
  44.6 14.1 %collective-permute-start.7 = (bf16[256,512]{1,0:T(8,128)(2,1)S(1)}, bf16[256,512]{1,0:T(8,128)(2,1)S(1)}, u32[]{:S(2)}, u32[]{:S(2)}) collective-permute-start(bf16[256,512]{1,0:T(8,128)(2,1)S(1)} %collective-permute-done.5), channel_id=1, source_target_pairs={{0,112},{8,120},{16,0},{24,8},{32,16},{40,24},{48,32},{56,40},{64,... | collective-permute-start | bytes 786440 | tf_op jit(solution)/shard_map/ppermute | solution.py:183
  50.1 13.0 %collective-permute-start.6 = (bf16[256,512]{1,0:T(8,128)(2,1)S(1)}, bf16[256,512]{1,0:T(8,128)(2,1)S(1)}, u32[]{:S(2)}, u32[]{:S(2)}) collective-permute-start(bf16[256,512]{1,0:T(8,128)(2,1)S(1)} %collective-permute-done.4), channel_id=1, source_target_pairs={{0,16},{8,24},{16,32},{24,40},{32,48},{40,56},{48,64},{56,72},{64,... | collective-permute-start | bytes 786440 | tf_op jit(solution)/shard_map/ppermute | solution.py:183
  52.1 20.9 %copy-start.2 = (bf16[1280,512]{1,0:T(8,128)(2,1)}, bf16[1280,512]{1,0:T(8,128)(2,1)S(1)}, u32[]{:S(2)}) copy-start(bf16[1280,512]{1,0:T(8,128)(2,1)S(1)} %constant_dynamic-update-slice_fusion) | copy-start | bytes 3932164
  52.1 27.0 %collective-permute-start.11 = (bf16[1280,512]{1,0:T(8,128)(2,1)S(1)}, bf16[1280,512]{1,0:T(8,128)(2,1)}, u32[]{:S(2)}, u32[]{:S(2)}) collective-permute-start(bf16[1280,512]{1,0:T(8,128)(2,1)S(1)} %constant_dynamic-update-slice_fusion), channel_id=1, source_target_pairs={{0,8},{8,0},{16,24},{24,16},{32,40},{40,32},{48,56},{56,48},{64,72... | collective-permute-start | bytes 3932168 | tf_op jit(solution)/shard_map/ppermute | solution.py:183
  58.7 6.3 %collective-permute-start.8 = (bf16[80,640]{1,0:T(8,128)(2,1)S(1)}, bf16[80,640]{1,0:T(8,128)(2,1)S(1)}, u32[]{:S(2)}, u32[]{:S(2)}) collective-permute-start(bf16[80,640]{1,0:T(8,128)(2,1)S(1)} %copy-done.5), channel_id=1, source_target_pairs={{0,8},{8,16},{16,24},{24,32},{32,40},{40,48},{48,56},{56,64},{64,7... | collective-permute-start | bytes 307208 | tf_op jit(solution)/shard_map/ppermute | solution.py:268
  60.7 6.4 %collective-permute-start.9 = (bf16[80,640]{1,0:T(8,128)(2,1)S(1)}, bf16[80,640]{1,0:T(8,128)(2,1)S(1)}, u32[]{:S(2)}, u32[]{:S(2)}) collective-permute-start(bf16[80,640]{1,0:T(8,128)(2,1)S(1)} %copy-done.4), channel_id=1, source_target_pairs={{8,0},{16,8},{24,16},{32,24},{40,32},{48,40},{56,48},{64,56},{72,6... | collective-permute-start | bytes 307208 | tf_op jit(solution)/shard_map/ppermute | solution.py:269
  63.1 9.8 %collective-permute-start.10 = (bf16[256,512]{1,0:T(8,128)(2,1)S(1)}, bf16[256,512]{1,0:T(8,128)(2,1)S(1)}, u32[]{:S(2)}, u32[]{:S(2)}) collective-permute-start(bf16[256,512]{1,0:T(8,128)(2,1)S(1)} %collective-permute-done.6), channel_id=1, source_target_pairs={{0,16},{8,24},{16,32},{24,40},{32,48},{40,56},{48,64},{56,72},{64,... | collective-permute-start | bytes 786440 | tf_op jit(solution)/shard_map/ppermute | solution.py:183
  65.0 2.0 %copy-start.6 = (bf16[80,640]{1,0:T(8,128)(2,1)}, bf16[80,640]{1,0:T(8,128)(2,1)S(1)}, u32[]{:S(2)}) copy-start(bf16[80,640]{1,0:T(8,128)(2,1)S(1)} %collective-permute-done.8.low_ref) | copy-start | bytes 307204
  67.0 0.6 copy-start.7
  73.0 6.1 %copy-start.1 = (bf16[768,512]{1,0:T(8,128)(2,1)}, bf16[768,512]{1,0:T(8,128)(2,1)S(1)}, u32[]{:S(2)}) copy-start(bf16[768,512]{1,0:T(8,128)(2,1)S(1)} %constant_dynamic-update-slice_fusion.5) | copy-start | bytes 2359300
  73.0 6.1 %collective-permute-start.12 = (bf16[768,512]{1,0:T(8,128)(2,1)S(1)}, bf16[768,512]{1,0:T(8,128)(2,1)S(1)}, u32[]{:S(2)}, u32[]{:S(2)}) collective-permute-start(bf16[768,512]{1,0:T(8,128)(2,1)S(1)} %constant_dynamic-update-slice_fusion.5), channel_id=1, source_target_pairs={{0,8},{8,0},{16,24},{24,16},{32,40},{40,32},{48,56},{56,48},{64,72... | collective-permute-start | bytes 2359304 | tf_op jit(solution)/shard_map/ppermute | solution.py:183
  79.0 1.0 %copy-start.3 = (bf16[768,512]{1,0:T(8,128)(2,1)}, bf16[768,512]{1,0:T(8,128)(2,1)S(1)}, u32[]{:S(2)}) copy-start(bf16[768,512]{1,0:T(8,128)(2,1)S(1)} %collective-permute-done.12) | copy-start | bytes 2359300
Sparse Core Ops, SparseCore 0:
  10.1 62.6 all-gather.2

commit v3 on v2

--- a/solution.py
+++ b/solution.py
@@ -279,7 +279,7 @@
         name="receive_rows",
     )(first, dest_row[None], attn_out, stats, from_low, from_high)
     far = jnp.concatenate([up3, after(down3, attn_packed, stats_packed), up4], axis=0)
-    far_other = move(far, other)
+    far_other = move(after(far, all_grad), other)
     pieces = [piece.reshape(-1, X, *out_weight.shape) for piece in (near, far, near_other, far_other)]
 
     return attend(place, all_grad, *pieces, queries, keys, values, attn_packed, stats_packed)

time: 97.3 us -> 99.2 us (1.020)
  starting transfers between devices: 53 us -> 54.2 us
    ppermute x11, waiting for transfers between devices: 7.46 us -> 10 us  [move(): return lax.ppermute(block, 'dp', pairs)]
    ppermute x1, waiting for transfers between devices: 1.98 us -> 0.01 us  [on_device(): from_high = lax.ppermute(to_low, 'dp', [(b, a) for a, b in forward])]
  transfers between devices with their start and end apart: 14 -> 14, of which waited for: 6 -> 5; matrix products, arithmetic and copies ran while one was open for 2% -> 2% of each run, Pallas kernels for 6% -> 6%
where the time goes in v3:
time: 99.2 us; the launch traced here: 98.6 us
  starting transfers between devices  54.2 us (55%)
  Pallas kernels  15.9 us (16%)
  between operations  14.4 us (15%)
  waiting for transfers between devices  10.7 us (11%)
  local copies, waits for them, and re-layouts  1.8 us (2%)
  other arithmetic  1.52 us (2%)
    ppermute x11, starting transfers between devices, move(): return lax.ppermute(block, 'dp', pairs)  49.1 us
    ppermute x11, waiting for transfers between devices, move(): return lax.ppermute(block, 'dp', pairs)  10 us
    pallas_call x1, Pallas kernels, attend(): pl.pallas_call(attend_kernel, out_shape=(jax.ShapeDtypeStruct((rows, widt...  9.85 us
    pallas_call x1, Pallas kernels, on_device(): pl.pallas_call(receive_kernel, out_shape=(jax.ShapeDtypeStruct((rows, wid...  3.49 us
    ppermute x1, starting transfers between devices, on_device(): from_high = lax.ppermute(to_low, 'dp', [(b, a) for a, b in forward])  2.8 us
    pallas_call x1, Pallas kernels, on_device(): pl.pallas_call(send_kernel, out_shape=(message, message, jax.ShapeDtypeSt...  2.56 us
    ppermute x1, starting transfers between devices, on_device(): from_low = lax.ppermute(to_high, 'dp', forward)  2.26 us
  transfers between devices with their start and end apart: 14, of which 5 were waited for; matrix products, arithmetic and copies ran while one was open for 2% of the time, Pallas kernels for 6%

profile of v3, /device:TPU:1, one launch (start us, length us, event | category | flops | bytes accessed | tf_op | source)
XLA Modules:
  0.0 98.6 jit_solution(10380815746132026694)
XLA Ops:
  7.2 0.0 copy-start
  7.2 0.0 all-gather.3.cloned.1.call-start
  7.2 0.7 all-gather.3.cloned.1.call-update
  7.9 3.9 %collective-permute-start = (bf16[64,512]{1,0:T(8,128)(2,1)}, bf16[64,512]{1,0:T(8,128)(2,1)S(1)}, u32[]{:S(2)}, u32[]{:S(2)}) collective-permute-start(bf16[64,512]{1,0:T(8,128)(2,1)} %param.15), channel_id=1, source_target_pairs={{0,128},{8,136},{16,144},{24,152},{32,160},{40,168},{48,176},{56,1... | collective-permute-start | bytes 196616 | tf_op jit(solution)/shard_map/ppermute | solution.py:183
  11.9 1.9 %collective-permute-done = bf16[64,512]{1,0:T(8,128)(2,1)S(1)} collective-permute-done((bf16[64,512]{1,0:T(8,128)(2,1)}, bf16[64,512]{1,0:T(8,128)(2,1)S(1)}, u32[]{:S(2)}, u32[]{:S(2)}) %collective-permute-start) | collective-permute-done | bytes 65568 | tf_op jit(solution)/shard_map/ppermute | solution.py:183
  13.7 0.8 pad_maximum_fusion.1
  14.6 4.6 %collective-permute-start.1 = (bf16[128,512]{1,0:T(8,128)(2,1)S(1)}, bf16[128,512]{1,0:T(8,128)(2,1)S(1)}, u32[]{:S(2)}, u32[]{:S(2)}) collective-permute-start(bf16[128,512]{1,0:T(8,128)(2,1)S(1)} %pad_maximum_fusion.1), channel_id=1, source_target_pairs={{0,384},{8,392},{16,400},{24,408},{32,416},{40,424},{48,432},{56,4... | collective-permute-start | bytes 393224 | tf_op jit(solution)/shard_map/ppermute | solution.py:183
  19.2 2.6 %send_rows.1 = (bf16[80,640]{1,0:T(8,128)(2,1)}, bf16[80,640]{1,0:T(8,128)(2,1)}, bf16[128,512]{1,0:T(8,128)(2,1)}) custom-call(s32[1]{0:T(128)} %bitcast.4.first_ref, s32[1,512]{1,0:T(1,128)} %bitcast.14, s32[1,512]{1,0:T(1,128)} %bitcast.15, f32[4,512]{1,0:T(4,128)} %norm_ref.1, bf16[512,512]{1,0:T(8,128)(2,1)} %attn_ref.3), custom_call_target="tpu_custom_call" | custom-call | flops 104857600 | bytes 1048576 | tf_op jit(solution)/shard_map/send_rows/pallas_call | solution.py:243
  21.8 0.0 collective-permute-done.1
  21.8 0.0 copy-done
  21.8 0.0 copy-start.5
  21.8 0.0 copy-start.4
  21.8 4.1 %collective-permute-start.2 = (bf16[256,512]{1,0:T(8,128)(2,1)S(1)}, bf16[256,512]{1,0:T(8,128)(2,1)S(1)}, u32[]{:S(2)}, u32[]{:S(2)}) collective-permute-start(bf16[256,512]{1,0:T(8,128)(2,1)S(1)} %pad_maximum_fusion), channel_id=1, source_target_pairs={{0,16},{8,24},{16,32},{24,40},{32,48},{40,56},{48,64},{56,72},{64,... | collective-permute-start | bytes 786440 | tf_op jit(solution)/shard_map/ppermute | solution.py:183
  26.0 8.6 %collective-permute-start.3 = (bf16[256,512]{1,0:T(8,128)(2,1)S(1)}, bf16[256,512]{1,0:T(8,128)(2,1)S(1)}, u32[]{:S(2)}, u32[]{:S(2)}) collective-permute-start(bf16[256,512]{1,0:T(8,128)(2,1)S(1)} %pad_maximum_fusion), channel_id=1, source_target_pairs={{0,112},{8,120},{16,0},{24,8},{32,16},{40,24},{48,32},{56,40},{64,... | collective-permute-start | bytes 786440 | tf_op jit(solution)/shard_map/ppermute | solution.py:183
  34.6 2.2 %collective-permute-done.2 = bf16[256,512]{1,0:T(8,128)(2,1)S(1)} collective-permute-done((bf16[256,512]{1,0:T(8,128)(2,1)S(1)}, bf16[256,512]{1,0:T(8,128)(2,1)S(1)}, u32[]{:S(2)}, u32[]{:S(2)}) %collective-permute-start.2) | collective-permute-done | bytes 262176 | tf_op jit(solution)/shard_map/ppermute | solution.py:183
  36.8 1.9 %collective-permute-start.4 = (bf16[256,512]{1,0:T(8,128)(2,1)S(1)}, bf16[256,512]{1,0:T(8,128)(2,1)S(1)}, u32[]{:S(2)}, u32[]{:S(2)}) collective-permute-start(bf16[256,512]{1,0:T(8,128)(2,1)S(1)} %collective-permute-done.2), channel_id=1, source_target_pairs={{0,16},{8,24},{16,32},{24,40},{32,48},{40,56},{48,64},{56,72},{64,... | collective-permute-start | bytes 786440 | tf_op jit(solution)/shard_map/ppermute | solution.py:183
  38.7 0.0 collective-permute-done.3
  38.7 4.6 %collective-permute-start.5 = (bf16[256,512]{1,0:T(8,128)(2,1)S(1)}, bf16[256,512]{1,0:T(8,128)(2,1)S(1)}, u32[]{:S(2)}, u32[]{:S(2)}) collective-permute-start(bf16[256,512]{1,0:T(8,128)(2,1)S(1)} %collective-permute-done.3), channel_id=1, source_target_pairs={{0,112},{8,120},{16,0},{24,8},{32,16},{40,24},{48,32},{56,40},{64,... | collective-permute-start | bytes 786440 | tf_op jit(solution)/shard_map/ppermute | solution.py:183
  43.4 2.1 %collective-permute-done.4 = bf16[256,512]{1,0:T(8,128)(2,1)S(1)} collective-permute-done((bf16[256,512]{1,0:T(8,128)(2,1)S(1)}, bf16[256,512]{1,0:T(8,128)(2,1)S(1)}, u32[]{:S(2)}, u32[]{:S(2)}) %collective-permute-start.4) | collective-permute-done | bytes 262176 | tf_op jit(solution)/shard_map/ppermute | solution.py:183
  45.5 1.9 %collective-permute-start.6 = (bf16[256,512]{1,0:T(8,128)(2,1)S(1)}, bf16[256,512]{1,0:T(8,128)(2,1)S(1)}, u32[]{:S(2)}, u32[]{:S(2)}) collective-permute-start(bf16[256,512]{1,0:T(8,128)(2,1)S(1)} %collective-permute-done.4), channel_id=1, source_target_pairs={{0,16},{8,24},{16,32},{24,40},{32,48},{40,56},{48,64},{56,72},{64,... | collective-permute-start | bytes 786440 | tf_op jit(solution)/shard_map/ppermute | solution.py:183
  47.4 0.0 collective-permute-done.5
  47.4 4.6 %collective-permute-start.7 = (bf16[256,512]{1,0:T(8,128)(2,1)S(1)}, bf16[256,512]{1,0:T(8,128)(2,1)S(1)}, u32[]{:S(2)}, u32[]{:S(2)}) collective-permute-start(bf16[256,512]{1,0:T(8,128)(2,1)S(1)} %collective-permute-done.5), channel_id=1, source_target_pairs={{0,112},{8,120},{16,0},{24,8},{32,16},{40,24},{48,32},{56,40},{64,... | collective-permute-start | bytes 786440 | tf_op jit(solution)/shard_map/ppermute | solution.py:183
  52.1 0.0 copy-start.2
  52.1 6.6 %collective-permute-start.11 = (bf16[1280,512]{1,0:T(8,128)(2,1)S(1)}, bf16[1280,512]{1,0:T(8,128)(2,1)}, u32[]{:S(2)}, u32[]{:S(2)}) collective-permute-start(bf16[1280,512]{1,0:T(8,128)(2,1)S(1)} %constant_dynamic-update-slice_fusion), channel_id=1, source_target_pairs={{0,8},{8,0},{16,24},{24,16},{32,40},{40,32},{48,56},{56,48},{64,72... | collective-permute-start | bytes 3932168 | tf_op jit(solution)/shard_map/ppermute | solution.py:183
  58.7 0.0 collective-permute-done.7
  58.7 0.0 copy-done.5
  58.7 2.3 %collective-permute-start.8 = (bf16[80,640]{1,0:T(8,128)(2,1)S(1)}, bf16[80,640]{1,0:T(8,128)(2,1)S(1)}, u32[]{:S(2)}, u32[]{:S(2)}) collective-permute-start(bf16[80,640]{1,0:T(8,128)(2,1)S(1)} %copy-done.5), channel_id=1, source_target_pairs={{0,8},{8,16},{16,24},{24,32},{32,40},{40,48},{48,56},{56,64},{64,7... | collective-permute-start | bytes 307208 | tf_op jit(solution)/shard_map/ppermute | solution.py:268
  61.0 0.0 copy-done.4
  61.0 2.8 %collective-permute-start.9 = (bf16[80,640]{1,0:T(8,128)(2,1)S(1)}, bf16[80,640]{1,0:T(8,128)(2,1)S(1)}, u32[]{:S(2)}, u32[]{:S(2)}) collective-permute-start(bf16[80,640]{1,0:T(8,128)(2,1)S(1)} %copy-done.4), channel_id=1, source_target_pairs={{8,0},{16,8},{24,16},{32,24},{40,32},{48,40},{56,48},{64,56},{72,6... | collective-permute-start | bytes 307208 | tf_op jit(solution)/shard_map/ppermute | solution.py:269
  63.8 0.0 collective-permute-done.6
  63.8 4.0 %collective-permute-start.10 = (bf16[256,512]{1,0:T(8,128)(2,1)S(1)}, bf16[256,512]{1,0:T(8,128)(2,1)S(1)}, u32[]{:S(2)}, u32[]{:S(2)}) collective-permute-start(bf16[256,512]{1,0:T(8,128)(2,1)S(1)} %collective-permute-done.6), channel_id=1, source_target_pairs={{0,16},{8,24},{16,32},{24,40},{32,48},{40,56},{48,64},{56,72},{64,... | collective-permute-start | bytes 786440 | tf_op jit(solution)/shard_map/ppermute | solution.py:183
  67.8 0.0 collective-permute-done.8.low_ref
  67.8 0.0 copy-start.6
  67.8 0.0 collective-permute-done.9.high_ref
  67.9 0.0 copy-start.7
  67.9 0.6 copy-done.6
  68.5 0.0 copy-done.7
  68.5 3.5 %receive_rows.1 = (bf16[512,512]{1,0:T(8,128)(2,1)}, f32[16,512]{1,0:T(8,128)}) custom-call(s32[1]{0:T(128)} %bitcast.4.first_ref, s32[1,512]{1,0:T(1,128)} %bitcast.18, bf16[512,512]{1,0:T(8,128)(2,1)} %attn_ref.3, bf16[128,512]{1,0:T(8,128)(2,1)} %get-tuple-element.16.stats_ref, bf16[80,640]{1,0:T(8,128)(2,1)} %copy-done.6, bf16[80,640]{1,0:T(8,128)(2,1)} %copy-done.7), custom_call_target="tpu_custom_call" | custom-call | flops 335544320 | bytes 2097152 | tf_op jit(solution)/shard_map/receive_rows/pallas_call | solution.py:270
  72.0 2.6 %collective-permute-done.10 = bf16[256,512]{1,0:T(8,128)(2,1)S(1)} collective-permute-done((bf16[256,512]{1,0:T(8,128)(2,1)S(1)}, bf16[256,512]{1,0:T(8,128)(2,1)S(1)}, u32[]{:S(2)}, u32[]{:S(2)}) %collective-permute-start.10) | collective-permute-done | bytes 262176 | tf_op jit(solution)/shard_map/ppermute | solution.py:183
  74.7 0.0 copy-done.2
  74.7 0.0 copy-start.1
  74.7 0.0 all-gather.3.cloned.1.call-done
  74.7 4.3 %collective-permute-start.12 = (bf16[768,512]{1,0:T(8,128)(2,1)S(1)}, bf16[768,512]{1,0:T(8,128)(2,1)S(1)}, u32[]{:S(2)}, u32[]{:S(2)}) collective-permute-start(bf16[768,512]{1,0:T(8,128)(2,1)S(1)} %constant_dynamic-update-slice_fusion.5), channel_id=1, source_target_pairs={{0,8},{8,0},{16,24},{24,16},{32,40},{40,32},{48,56},{56,48},{64,72... | collective-permute-start | bytes 2359304 | tf_op jit(solution)/shard_map/ppermute | solution.py:183
  79.0 0.7 pad_add_fusion.me_ref
  79.7 0.0 collective-permute-done.11
  79.7 1.2 %collective-permute-done.12 = bf16[768,512]{1,0:T(8,128)(2,1)S(1)} collective-permute-done((bf16[768,512]{1,0:T(8,128)(2,1)S(1)}, bf16[768,512]{1,0:T(8,128)(2,1)S(1)}, u32[]{:S(2)}, u32[]{:S(2)}) %collective-permute-start.12) | collective-permute-done | bytes 786464 | tf_op jit(solution)/shard_map/ppermute | solution.py:183
  80.9 1.0 copy-done.3
  81.9 9.9 %attend.1 = (bf16[512,512]{1,0:T(8,128)(2,1)}, bf16[512,128]{1,0:T(8,128)(2,1)}, bf16[512,128]{1,0:T(8,128)(2,1)}) custom-call(s32[3]{0:T(128)} %pad_add_fusion.me_ref, bf16[8,512,512]{2,1,0:T(8,128)(2,1)} %bitcast.16, bf16[5,4,64,512]{3,2,1,0:T(8,128)(2,1)} %bitcast.13, bf16[3,4,64,512]{3,2,1,0:T(8,128)(2,1)} %bitcast.12, ...), custom_call_target="tpu_custom_call" | custom-call | flops 4294967296 | bytes 12582912 | tf_op jit(solution)/shard_map/attend/pallas_call | solution.py:202
  (11 shorter events, 0.2 us)
Async XLA Ops:
  7.2 14.6 %copy-start = (bf16[64,512]{1,0:T(8,128)(2,1)S(1)}, bf16[64,512]{1,0:T(8,128)(2,1)}, u32[]{:S(2)}) copy-start(bf16[64,512]{1,0:T(8,128)(2,1)} %param.15) | copy-start | bytes 196612
  7.2 67.5 %all-gather.3.cloned.1.call-start = ((), (), s32[]{:S(2)}) async-start(), calls=%async_computation | async-start | bytes 4718592 | tf_op jit(solution)/shard_map/all_gather | solution.py:237
  7.9 5.8 %collective-permute-start = (bf16[64,512]{1,0:T(8,128)(2,1)}, bf16[64,512]{1,0:T(8,128)(2,1)S(1)}, u32[]{:S(2)}, u32[]{:S(2)}) collective-permute-start(bf16[64,512]{1,0:T(8,128)(2,1)} %param.15), channel_id=1, source_target_pairs={{0,128},{8,136},{16,144},{24,152},{32,160},{40,168},{48,176},{56,1... | collective-permute-start | bytes 196616 | tf_op jit(solution)/shard_map/ppermute | solution.py:183
  14.6 7.2 %collective-permute-start.1 = (bf16[128,512]{1,0:T(8,128)(2,1)S(1)}, bf16[128,512]{1,0:T(8,128)(2,1)S(1)}, u32[]{:S(2)}, u32[]{:S(2)}) collective-permute-start(bf16[128,512]{1,0:T(8,128)(2,1)S(1)} %pad_maximum_fusion.1), channel_id=1, source_target_pairs={{0,384},{8,392},{16,400},{24,408},{32,416},{40,424},{48,432},{56,4... | collective-permute-start | bytes 393224 | tf_op jit(solution)/shard_map/ppermute | solution.py:183
  21.8 36.9 %copy-start.5 = (bf16[80,640]{1,0:T(8,128)(2,1)S(1)}, bf16[80,640]{1,0:T(8,128)(2,1)}, u32[]{:S(2)}) copy-start(bf16[80,640]{1,0:T(8,128)(2,1)} %get-tuple-element.17) | copy-start | bytes 307204
  21.8 39.2 %copy-start.4 = (bf16[80,640]{1,0:T(8,128)(2,1)S(1)}, bf16[80,640]{1,0:T(8,128)(2,1)}, u32[]{:S(2)}) copy-start(bf16[80,640]{1,0:T(8,128)(2,1)} %get-tuple-element.18) | copy-start | bytes 307204
  21.8 15.0 %collective-permute-start.2 = (bf16[256,512]{1,0:T(8,128)(2,1)S(1)}, bf16[256,512]{1,0:T(8,128)(2,1)S(1)}, u32[]{:S(2)}, u32[]{:S(2)}) collective-permute-start(bf16[256,512]{1,0:T(8,128)(2,1)S(1)} %pad_maximum_fusion), channel_id=1, source_target_pairs={{0,16},{8,24},{16,32},{24,40},{32,48},{40,56},{48,64},{56,72},{64,... | collective-permute-start | bytes 786440 | tf_op jit(solution)/shard_map/ppermute | solution.py:183
  26.0 12.7 %collective-permute-start.3 = (bf16[256,512]{1,0:T(8,128)(2,1)S(1)}, bf16[256,512]{1,0:T(8,128)(2,1)S(1)}, u32[]{:S(2)}, u32[]{:S(2)}) collective-permute-start(bf16[256,512]{1,0:T(8,128)(2,1)S(1)} %pad_maximum_fusion), channel_id=1, source_target_pairs={{0,112},{8,120},{16,0},{24,8},{32,16},{40,24},{48,32},{56,40},{64,... | collective-permute-start | bytes 786440 | tf_op jit(solution)/shard_map/ppermute | solution.py:183
  36.8 8.7 %collective-permute-start.4 = (bf16[256,512]{1,0:T(8,128)(2,1)S(1)}, bf16[256,512]{1,0:T(8,128)(2,1)S(1)}, u32[]{:S(2)}, u32[]{:S(2)}) collective-permute-start(bf16[256,512]{1,0:T(8,128)(2,1)S(1)} %collective-permute-done.2), channel_id=1, source_target_pairs={{0,16},{8,24},{16,32},{24,40},{32,48},{40,56},{48,64},{56,72},{64,... | collective-permute-start | bytes 786440 | tf_op jit(solution)/shard_map/ppermute | solution.py:183
  38.7 8.7 %collective-permute-start.5 = (bf16[256,512]{1,0:T(8,128)(2,1)S(1)}, bf16[256,512]{1,0:T(8,128)(2,1)S(1)}, u32[]{:S(2)}, u32[]{:S(2)}) collective-permute-start(bf16[256,512]{1,0:T(8,128)(2,1)S(1)} %collective-permute-done.3), channel_id=1, source_target_pairs={{0,112},{8,120},{16,0},{24,8},{32,16},{40,24},{48,32},{56,40},{64,... | collective-permute-start | bytes 786440 | tf_op jit(solution)/shard_map/ppermute | solution.py:183
  45.5 18.3 %collective-permute-start.6 = (bf16[256,512]{1,0:T(8,128)(2,1)S(1)}, bf16[256,512]{1,0:T(8,128)(2,1)S(1)}, u32[]{:S(2)}, u32[]{:S(2)}) collective-permute-start(bf16[256,512]{1,0:T(8,128)(2,1)S(1)} %collective-permute-done.4), channel_id=1, source_target_pairs={{0,16},{8,24},{16,32},{24,40},{32,48},{40,56},{48,64},{56,72},{64,... | collective-permute-start | bytes 786440 | tf_op jit(solution)/shard_map/ppermute | solution.py:183
  47.4 11.3 %collective-permute-start.7 = (bf16[256,512]{1,0:T(8,128)(2,1)S(1)}, bf16[256,512]{1,0:T(8,128)(2,1)S(1)}, u32[]{:S(2)}, u32[]{:S(2)}) collective-permute-start(bf16[256,512]{1,0:T(8,128)(2,1)S(1)} %collective-permute-done.5), channel_id=1, source_target_pairs={{0,112},{8,120},{16,0},{24,8},{32,16},{40,24},{48,32},{56,40},{64,... | collective-permute-start | bytes 786440 | tf_op jit(solution)/shard_map/ppermute | solution.py:183
  52.1 22.6 %copy-start.2 = (bf16[1280,512]{1,0:T(8,128)(2,1)}, bf16[1280,512]{1,0:T(8,128)(2,1)S(1)}, u32[]{:S(2)}) copy-start(bf16[1280,512]{1,0:T(8,128)(2,1)S(1)} %constant_dynamic-update-slice_fusion) | copy-start | bytes 3932164
  52.1 27.6 %collective-permute-start.11 = (bf16[1280,512]{1,0:T(8,128)(2,1)S(1)}, bf16[1280,512]{1,0:T(8,128)(2,1)}, u32[]{:S(2)}, u32[]{:S(2)}) collective-permute-start(bf16[1280,512]{1,0:T(8,128)(2,1)S(1)} %constant_dynamic-update-slice_fusion), channel_id=1, source_target_pairs={{0,8},{8,0},{16,24},{24,16},{32,40},{40,32},{48,56},{56,48},{64,72... | collective-permute-start | bytes 3932168 | tf_op jit(solution)/shard_map/ppermute | solution.py:183
  58.7 9.1 %collective-permute-start.8 = (bf16[80,640]{1,0:T(8,128)(2,1)S(1)}, bf16[80,640]{1,0:T(8,128)(2,1)S(1)}, u32[]{:S(2)}, u32[]{:S(2)}) collective-permute-start(bf16[80,640]{1,0:T(8,128)(2,1)S(1)} %copy-done.5), channel_id=1, source_target_pairs={{0,8},{8,16},{16,24},{24,32},{32,40},{40,48},{48,56},{56,64},{64,7... | collective-permute-start | bytes 307208 | tf_op jit(solution)/shard_map/ppermute | solution.py:268
  61.0 6.9 %collective-permute-start.9 = (bf16[80,640]{1,0:T(8,128)(2,1)S(1)}, bf16[80,640]{1,0:T(8,128)(2,1)S(1)}, u32[]{:S(2)}, u32[]{:S(2)}) collective-permute-start(bf16[80,640]{1,0:T(8,128)(2,1)S(1)} %copy-done.4), channel_id=1, source_target_pairs={{8,0},{16,8},{24,16},{32,24},{40,32},{48,40},{56,48},{64,56},{72,6... | collective-permute-start | bytes 307208 | tf_op jit(solution)/shard_map/ppermute | solution.py:269
  63.8 10.8 %collective-permute-start.10 = (bf16[256,512]{1,0:T(8,128)(2,1)S(1)}, bf16[256,512]{1,0:T(8,128)(2,1)S(1)}, u32[]{:S(2)}, u32[]{:S(2)}) collective-permute-start(bf16[256,512]{1,0:T(8,128)(2,1)S(1)} %collective-permute-done.6), channel_id=1, source_target_pairs={{0,16},{8,24},{16,32},{24,40},{32,48},{40,56},{48,64},{56,72},{64,... | collective-permute-start | bytes 786440 | tf_op jit(solution)/shard_map/ppermute | solution.py:183
  67.8 0.6 copy-start.6
  67.9 0.7 copy-start.7
  74.7 6.2 %copy-start.1 = (bf16[768,512]{1,0:T(8,128)(2,1)}, bf16[768,512]{1,0:T(8,128)(2,1)S(1)}, u32[]{:S(2)}) copy-start(bf16[768,512]{1,0:T(8,128)(2,1)S(1)} %constant_dynamic-update-slice_fusion.5) | copy-start | bytes 2359300
  74.7 6.2 %collective-permute-start.12 = (bf16[768,512]{1,0:T(8,128)(2,1)S(1)}, bf16[768,512]{1,0:T(8,128)(2,1)S(1)}, u32[]{:S(2)}, u32[]{:S(2)}) collective-permute-start(bf16[768,512]{1,0:T(8,128)(2,1)S(1)} %constant_dynamic-update-slice_fusion.5), channel_id=1, source_target_pairs={{0,8},{8,0},{16,24},{24,16},{32,40},{40,32},{48,56},{56,48},{64,72... | collective-permute-start | bytes 2359304 | tf_op jit(solution)/shard_map/ppermute | solution.py:183
  80.9 1.0 copy-start.3
Sparse Core Ops, SparseCore 0:
  10.1 62.6 all-gather.2
